TPU v7x, 512 devices: a whole 4x4x16 slice. The times are simulated.
512 devices in a mesh: row: 32 (over x, z_hi, y), col: 16 (over z_lo, core).
Axes of the slice: x: 4, y: 4, z: 16 (z_hi: 2, z_lo: 8; z = z_hi * 8 + z_lo), core: 2. Of those that a mesh axis runs over, the one named last changes fastest.
Arguments:
- positions: float32 [3, 262144], P(None, ('row', 'col')), may hold values from 0 to 2.4
- vel_half: float32 [3, 262144], P(None, ('row', 'col')), may hold values from -1.2 to 1.2
- charges: float32 [262144], P(('row', 'col')), may hold values from -1 to 1
- types: int32 [262144], P(('row', 'col')), may hold values from 0 to 17
- six_table: float32 [18, 18], replicated, may hold values from 0.05 to 0.25
- twelve_table: float32 [18, 18], replicated, may hold values from 0.0005 to 0.003
- tile_pairs: int32 [32, 16, 2, 128], P('row', 'col'), may hold values from 0 to 127, as said below
- pair_counts: int32 [32, 16], P('row', 'col'), may hold values from 16 to 128, as said below
Outputs:
- positions_new: float32 [3, 262144], P(None, ('row', 'col'))
- force_new: float32 [3, 262144], P(None, ('row', 'col'))
- velocity_new: float32 [3, 262144], P(None, ('row', 'col'))
Inputs may be any that keep to these rules, and one draw needn't show every extreme that they name: `tile_pairs`: within one device's list all 128 slots are distinct tile pairs with indices in range of the two blocks; slots from pair_counts on hold valid pairs that are not used. Some device has a full list in every draw. `pair_counts`: each device's count is 128, 64, 32 or 16, and some device holds 128 in every draw.
All inputs are finite; a program needn't handle non-finite values.
Results may differ from a plain program's by a relative error of at most 0.0022.
Values sent between devices are 32-bit elements; how exact they have to be, the bound alone decides.
No kernel may reach another device: no remote copies, remote signals or barrier semaphores. Data moves between devices by JAX's collectives and lax.ppermute only.
A program may use at most 64 MiB of HBM per device.

v0:
```python
import jax
import jax.numpy as jnp
from jax import lax
from jax.sharding import PartitionSpec as P

TILE_ATOMS = 128
BEAD_TYPES = 18


TIME_STEP = 0.02
HALF_KICK = 0.01 / 72.0
SOFT_CORE = 0.5
COULOMB = 9.262364
REACTION = 0.28935185
INV_CUT_SQ = 1.0 / 1.44


def pair_forces(pos_i, pos_j, charge_i, charge_j, six_coef, twelve_coef, keep_pair):
    offset = pos_i[:, :, :, None] - pos_j[:, :, None, :]
    dist_sq = offset[0] * offset[0] + offset[1] * offset[1] + offset[2] * offset[2]
    soft_sq = dist_sq + SOFT_CORE
    inverse = 1.0 / soft_sq
    inverse_sq = inverse * inverse
    inverse_four = inverse_sq * inverse_sq
    dispersion = (
        12.0 * twelve_coef * inverse_four * inverse_sq * inverse - 6.0 * six_coef * inverse_four
    )
    coulomb = (
        COULOMB
        * charge_i[:, :, None]
        * charge_j[:, None, :]
        * (inverse * lax.rsqrt(soft_sq) - 2.0 * REACTION)
    )
    switch = jnp.maximum(1.0 - dist_sq * INV_CUT_SQ, 0.0)
    scalar = jnp.where(keep_pair, (dispersion + coulomb) * switch * switch, 0.0)
    product = scalar[None] * offset
    return (jnp.sum(product, axis=3), -jnp.sum(product, axis=2))


def split_three(values):
    upper = values.astype(jnp.bfloat16)
    rest = values - upper.astype(jnp.float32)
    middle = rest.astype(jnp.bfloat16)
    lower = (rest - middle.astype(jnp.float32)).astype(jnp.bfloat16)
    return [upper, middle, lower]


def shards(positions, vel_half, charges, types, six_table, twelve_table, tile_pairs, pair_counts):
    atoms_dev = positions.shape[1]
    tiles_dev = atoms_dev // TILE_ATOMS
    moved_pos = positions + TIME_STEP * vel_half
    packed = jnp.concatenate([moved_pos, charges[None], types.astype(jnp.float32)[None]], axis=0)
    row_atoms = lax.all_gather(packed, "col", axis=1, tiled=True)
    col_atoms = lax.all_gather(packed, "row", axis=1, tiled=True)
    row_tiles = row_atoms.shape[1] // TILE_ATOMS
    col_tiles = col_atoms.shape[1] // TILE_ATOMS
    row_pos = row_atoms[0:3].reshape(3, row_tiles, TILE_ATOMS)
    col_pos = col_atoms[0:3].reshape(3, col_tiles, TILE_ATOMS)
    row_charge = row_atoms[3].reshape(row_tiles, TILE_ATOMS)
    col_charge = col_atoms[3].reshape(col_tiles, TILE_ATOMS)
    type_grid = jnp.arange(BEAD_TYPES, dtype=jnp.float32)[:, None, None]
    row_hot = (row_atoms[4].reshape(row_tiles, TILE_ATOMS)[None] == type_grid).astype(jnp.float32)
    col_hot = (col_atoms[4].reshape(col_tiles, TILE_ATOMS)[None] == type_grid).astype(jnp.bfloat16)
    row_six = jnp.einsum("st,sna->tna", six_table, row_hot, precision=lax.Precision.HIGHEST)
    row_twelve = jnp.einsum("st,sna->tna", twelve_table, row_hot, precision=lax.Precision.HIGHEST)
    coef_parts = jnp.stack(split_three(row_six) + split_three(row_twelve))
    slot_table = tile_pairs[0, 0]
    live_count = pair_counts[0, 0]
    my_row = lax.axis_index("row")
    my_col = lax.axis_index("col")
    group_size = 2 * tiles_dev
    group_count = slot_table.shape[1] // group_size
    upper_pair = lax.broadcasted_iota(
        jnp.int32, (TILE_ATOMS, TILE_ATOMS), 0
    ) < lax.broadcasted_iota(jnp.int32, (TILE_ATOMS, TILE_ATOMS), 1)

    def accumulate(group_index, totals):
        row_force, col_force = totals
        group = lax.dynamic_slice_in_dim(slot_table, group_index * group_size, group_size, 1)
        first = group[0]
        second = group[1]
        slot_ids = group_index * group_size + jnp.arange(group_size, dtype=jnp.int32)
        is_live = slot_ids < live_count
        same_tile = (second // tiles_dev == my_row) & (
            first == my_col * tiles_dev + second % tiles_dev
        )
        keep_pair = is_live[:, None, None] & (
            jnp.logical_not(same_tile)[:, None, None] | upper_pair[None]
        )
        hot_j = col_hot[:, second]
        looked = jnp.einsum(
            "ptga,tgb->pgab", coef_parts[:, :, first], hot_j, preferred_element_type=jnp.float32
        )
        six_coef = looked[0] + looked[1] + looked[2]
        twelve_coef = looked[3] + looked[4] + looked[5]
        force_i, force_j = pair_forces(
            row_pos[:, first],
            col_pos[:, second],
            row_charge[first],
            col_charge[second],
            six_coef,
            twelve_coef,
            keep_pair,
        )
        return (row_force.at[:, first].add(force_i), col_force.at[:, second].add(force_j))

    initial = (
        jnp.zeros((3, row_tiles, TILE_ATOMS), jnp.float32),
        jnp.zeros((3, col_tiles, TILE_ATOMS), jnp.float32),
    )
    row_force, col_force = lax.fori_loop(0, group_count, accumulate, initial)
    row_share = lax.psum_scatter(
        row_force.reshape(3, row_tiles * TILE_ATOMS), "col", scatter_dimension=1, tiled=True
    )
    whole_sum = lax.psum(col_force.reshape(3, col_tiles * TILE_ATOMS), "row")
    col_share = lax.dynamic_slice_in_dim(whole_sum, my_row * atoms_dev, atoms_dev, 1)
    force_new = row_share + col_share
    velocity_new = vel_half + HALF_KICK * force_new
    return (moved_pos, force_new, velocity_new)


def solution(mesh):
    placed = (
        P(None, ("row", "col")),
        P(None, ("row", "col")),
        P(("row", "col")),
        P(("row", "col")),
        P(),
        P(),
        P("row", "col", None, None),
        P("row", "col"),
    )
    return jax.shard_map(
        shards,
        mesh=mesh,
        in_specs=placed,
        out_specs=(P(None, ("row", "col")), P(None, ("row", "col")), P(None, ("row", "col"))),
        check_vma=False,
    )
```

profile of v0, /device:TPU:8, one launch (start us, length us, event | category | flops | bytes accessed | tf_op | source)
XLA Modules:
  0.0 1106.0 jit_solution(8666243704610676275)
XLA Ops:
  10.2 37.2 %all_gather.7 = f32[5,8192]{1,0:T(8,128)S(1)} all-gather(f32[5,512]{1,0:T(8,128)S(1)} %pad_maximum_fusion), channel_id=1, replica_groups=mesh['row'=32,'col'=16] {'col'}, dimensions={1}, use_global_device_ids=true | all-gather | bytes 174080 | tf_op jit(solution)/shard_map/all_gather | solution.py:53
  47.4 148.3 %all_gather.6 = f32[5,16384]{1,0:T(8,128)S(1)} all-gather(f32[5,512]{1,0:T(8,128)S(1)} %pad_maximum_fusion), channel_id=1, replica_groups=mesh['row'=32,'col'=16] {'row'}, dimensions={1}, use_global_device_ids=true | all-gather | bytes 337920 | tf_op jit(solution)/shard_map/all_gather | solution.py:54
  205.2 313.2 %while.18 = (s32[]{:T(128)}, f32[3,64,128]{2,0,1:T(4,128)}, f32[3,128,128]{2,0,1:T(4,128)}, s32[2,128]{1,0:T(2,128)}, s32[]{:T(128)}, /*index=5*/s32[]{:T(128)},...) while((s32[]{:T(128)}, f32[3,64,128]{2,0,1:T(4,128)}, ...), condition=%wide.region_5.6_spmd.clone, body=%wide.region_0.5_spmd.clone.sunk | while | flops 35215620 | bytes 12211071 | solution.py:111
  207.6 2.3 gather_fusion
  217.8 2.1 fusion.49
  227.2 2.3 gather_fusion
  237.4 2.1 fusion.49
  246.7 2.3 gather_fusion
  256.9 2.1 fusion.49
  262.0 2.0 scatter_fusion
  266.3 2.3 gather_fusion
  276.5 2.1 fusion.49
  285.8 2.3 gather_fusion
  296.0 2.1 fusion.49
  299.2 2.0 scatter_fusion.1
  305.4 2.3 gather_fusion
  315.6 2.1 fusion.49
  324.9 2.3 gather_fusion
  335.1 2.1 fusion.49
  340.2 2.0 scatter_fusion
  344.5 2.3 gather_fusion
  354.7 2.1 fusion.49
  364.0 2.3 gather_fusion
  374.2 2.1 fusion.49
  383.6 2.3 gather_fusion
  393.8 2.1 fusion.49
  398.9 2.0 scatter_fusion
  403.2 2.3 gather_fusion
  413.4 2.1 fusion.49
  416.5 2.0 scatter_fusion.1
  418.5 2.0 scatter_fusion
  422.8 2.3 gather_fusion
  433.0 2.1 fusion.49
  442.4 2.3 gather_fusion
  452.6 2.1 fusion.49
  455.7 2.0 scatter_fusion.1
  462.0 2.3 gather_fusion
  472.2 2.1 fusion.49
  475.3 2.0 scatter_fusion.1
  477.3 2.0 scatter_fusion
  481.7 2.3 gather_fusion
  491.9 2.1 fusion.49
  501.2 2.3 gather_fusion
  511.4 2.1 fusion.49
  514.5 2.0 scatter_fusion.1
  518.4 3.4 copy.36
  522.5 110.1 %reduce-scatter.4.cloned.1.call-done = f32[512,3]{1,0:T(8,128)} async-done(((f32[8192,3]{1,0:T(8,128)}), f32[512,3]{1,0:T(8,128)}) %reduce-scatter.4.cloned.1.call-update) | async-done | bytes 6160
  633.7 463.6 %all-reduce.2.cloned.1.call-done = f32[3,16384]{1,0:T(4,128)} async-done(((f32[3,16384]{1,0:T(4,128)}), f32[3,16384]{1,0:T(4,128)}) %all-reduce.2.cloned.1.call-update) | async-done | bytes 196624 | tf_op jit(solution)/shard_map/psum | solution.py:115
  (307 shorter events, 236.9 us)
Async XLA Ops:
  8.0 189.9 %copy-start = (f32[18,18]{1,0:T(8,128)S(1)}, f32[18,18]{1,0:T(8,128)}, u32[]{:S(2)}) copy-start(f32[18,18]{1,0:T(8,128)} %param.14) | copy-start | bytes 3892
  8.0 624.6 %reduce-scatter.4.cloned.1.call-start = ((), (), s32[]{:S(2)}) async-start(), calls=%async_computation.2 | async-start | bytes 4456448
  9.5 187.0 %copy-start.1 = (f32[3,512]{1,0:T(4,128)}, f32[3,512]{1,0:T(4,128)S(1)}, u32[]{:S(2)}) copy-start(f32[3,512]{1,0:T(4,128)S(1)} %multiply_add_fusion.1) | copy-start | bytes 18436
  195.7 5.2 copy-start.3
  521.9 575.4 %copy-start.2 = (f32[3,512]{1,0:T(4,128)S(1)}, f32[3,512]{1,0:T(4,128)}, u32[]{:S(2)}) copy-start(f32[3,512]{1,0:T(4,128)} %param.11) | copy-start | bytes 18436
  521.9 575.4 %all-reduce.2.cloned.1.call-start = ((), (), s32[]{:S(2)}) async-start(), calls=%async_computation.1 | async-start | bytes 524288 | tf_op jit(solution)/shard_map/psum | solution.py:115
Sparse Core Ops, SparseCore 0:
  522.0 110.5 reduce-scatter.3
Sparse Core Ops, SparseCore 1:
  525.3 571.9 all-reduce.1
where the time goes:
time: 1110 us
  waiting for transfers between devices  574 us (52%)
  blocking collectives  186 us (17%)
  other arithmetic  173 us (16%)
  local copies, waits for them, and re-layouts  145 us (13%)
  between operations  15.5 us (1%)
  matrix products  12.4 us (1%)
    psum x1, waiting for transfers between devices, shards(): whole_sum = lax.psum(col_force.reshape(3, col_tiles * TILE_ATOMS), 'row')  464 us
    all_gather x1, blocking collectives, shards(): col_atoms = lax.all_gather(packed, 'row', axis=1, tiled=True)  148 us
    unnamed x3, waiting for transfers between devices  111 us
    all_gather x1, blocking collectives, shards(): row_atoms = lax.all_gather(packed, 'col', axis=1, tiled=True)  37.2 us
    gather x16, local copies, waits for them, and re-layouts, accumulate(): coef_parts[:, :, first]  36.4 us
    mul x16, other arithmetic, pair_forces(): product = scalar[None] * offset  33.9 us
    scatter-add x16, other arithmetic, accumulate(): row_force.at[:, first].add(force_i)  31.2 us
    scatter-add x16, other arithmetic, accumulate(): col_force.at[:, second].add(force_j)  31.1 us
  transfers between devices with their start and end apart: 2, of which 2 were waited for; matrix products, arithmetic and copies ran while one was open for 0% of the time, Pallas kernels for 0%

commit v1 on v0

v1 whole, which is shorter than its diff:
```python
import functools
import jax
import jax.numpy as jnp
from jax import lax
from jax.experimental import pallas as pl
from jax.experimental.pallas import tpu as pltpu
from jax.sharding import PartitionSpec as P

TILE_ATOMS = 128
BEAD_TYPES = 18
LANES = 128

TIME_STEP = 0.02
HALF_KICK = 0.01 / 72.0
SOFT_CORE = 0.5
COULOMB = 9.262364
REACTION = 0.28935185
CUT_SQ = 1.44
CENTRE = 1.2

X_SIZE = 4
ZH_SIZE = 2
Y_SIZE = 4
TYPE_ROWS = 24
UNROLL = 2


def split_three(values):
    upper = values.astype(jnp.bfloat16).astype(jnp.float32)
    rest = values - upper
    middle = rest.astype(jnp.bfloat16).astype(jnp.float32)
    return upper, middle, rest - middle


def pair_kernel(
    pairs_ref, count_ref, row_ref, col_ref, table_ref, row_force, col_force, lhs_ref
):
    row_tiles = row_ref.shape[0]
    tiles_dev = 4
    my_row = lax.axis_index("row")
    my_col = lax.axis_index("col")
    my_zh = (my_row // Y_SIZE) % ZH_SIZE
    f32 = jnp.float32
    sub8 = lax.broadcasted_iota(jnp.int32, (8, LANES), 0)
    type_rows = lax.broadcasted_iota(jnp.int32, (TYPE_ROWS, LANES), 0).astype(f32)
    lane = lax.broadcasted_iota(jnp.int32, (TILE_ATOMS, LANES), 1)
    is_charge = (lane % 8 == 5) & (lane < 32)
    is_dist = (lane % 8 != 5) & (lane < 32)
    is_six = (lane >= 32) & (lane < 80)
    is_twelve = lane >= 80
    scale = jnp.where(sub8 < 3, -2.0, jnp.where(sub8 == 5, COULOMB / CUT_SQ**2, 0.0)).astype(f32)

    row_force[...] = jnp.zeros(row_force.shape, f32)
    col_force[...] = jnp.zeros(col_force.shape, f32)

    def prepare(tile, carry):
        block = row_ref[tile]
        left = block * scale
        left = jnp.where(sub8 == 3, 1.0, left)
        left = jnp.where(sub8 == 4, block[3:4] + SOFT_CORE, left)
        upper, middle, _ = split_three(left)
        hot = (jnp.broadcast_to(block[6:7], (TYPE_ROWS, LANES)) == type_rows).astype(f32)
        coefs = jnp.dot(
            table_ref[...], hot.astype(jnp.bfloat16), preferred_element_type=f32
        )
        whole = jnp.concatenate([upper, upper, middle, middle, coefs], axis=0).T
        for part, keep in enumerate((is_dist, is_charge, is_six, is_twelve)):
            lhs_ref[tile, part * TILE_ATOMS : (part + 1) * TILE_ATOMS, :] = jnp.where(
                keep, whole, 0.0
            ).astype(jnp.bfloat16)
        return carry

    lax.fori_loop(0, row_tiles, prepare, 0)

    def one_pair(first, place, same):
        right = col_ref[place]
        left = row_ref[first]
        upper, middle, lower = split_three(right)
        hot = (jnp.broadcast_to(right[6:7], (TYPE_ROWS, LANES)) == type_rows).astype(f32)
        rhs = jnp.concatenate(
            [upper, middle, upper, middle, hot, hot, hot, hot], axis=0
        ).astype(jnp.bfloat16)
        looked = jnp.dot(lhs_ref[first], rhs, preferred_element_type=f32)
        soft_sq = looked[0:128]
        charge = looked[128:256]
        six = looked[256:384]
        twelve = looked[384:512]
        root = lax.rsqrt(soft_sq)
        inverse = root * root
        inverse_two = inverse * inverse
        inverse_four = inverse_two * inverse_two
        dispersion = inverse_four * (twelve * (inverse_two * inverse) - six)
        coulomb = charge * (inverse * root - 2.0 * REACTION)
        switch = jnp.maximum((CUT_SQ + SOFT_CORE) - soft_sq, 0.0)
        scalar = (dispersion + coulomb) * (switch * switch)
        if same is not None:
            at_i = lax.broadcasted_iota(jnp.int32, (TILE_ATOMS, LANES), 0)
            scalar = jnp.where((at_i < lane) | jnp.logical_not(same), scalar, 0.0)
        high = scalar.astype(jnp.bfloat16)
        low = (scalar - high.astype(f32)).astype(jnp.bfloat16)
        right_x = jnp.concatenate([upper, middle, lower, lower], axis=0).astype(jnp.bfloat16)
        left_x = jnp.concatenate([*split_three(left), jnp.zeros_like(left)], axis=0).astype(
            jnp.bfloat16
        )
        nt = (((1,), (1,)), ((), ()))
        nn = (((1,), (0,)), ((), ()))
        sums_i = lax.dot_general(right_x, high, nt, preferred_element_type=f32)
        sums_i += lax.dot_general(right_x, low, nt, preferred_element_type=f32)
        sums_j = lax.dot_general(left_x, high, nn, preferred_element_type=f32)
        sums_j += lax.dot_general(left_x, low, nn, preferred_element_type=f32)
        sums_i = sums_i[0:8] + sums_i[8:16] + sums_i[16:24]
        sums_j = sums_j[0:8] + sums_j[8:16] + sums_j[16:24]
        force_i = left * sums_i[4:5] - sums_i
        force_j = right * sums_j[4:5] - sums_j
        row_force[first] += force_i[0:4]
        col_force[place] += force_j[0:4]

    def step(index, carry):
        found = []
        for part in range(UNROLL):
            slot = index * UNROLL + part
            first = pairs_ref[0, 0, 0, slot]
            second = pairs_ref[0, 0, 1, slot]
            owner = second // tiles_dev
            same = (owner == my_row) & (first == my_col * tiles_dev + second % tiles_dev)
            far = ((owner // Y_SIZE) % ZH_SIZE + my_zh) % ZH_SIZE
            place = (
                ((owner // (Y_SIZE * ZH_SIZE)) * Y_SIZE + owner % Y_SIZE) * ZH_SIZE + far
            ) * tiles_dev + second % tiles_dev
            found.append((first, place, same))
        any_same = functools.reduce(jnp.logical_or, [same for _, _, same in found])

        @pl.when(any_same)
        def _():
            for first, place, same in found:
                one_pair(first, place, same)

        @pl.when(jnp.logical_not(any_same))
        def _():
            for first, place, _ in found:
                one_pair(first, place, None)

        return carry

    lax.fori_loop(0, count_ref[0, 0] // UNROLL, step, 0)


def shards(positions, vel_half, charges, types, six_table, twelve_table, tile_pairs, pair_counts):
    atoms_dev = positions.shape[1]
    tiles_dev = atoms_dev // TILE_ATOMS
    n_row = X_SIZE * ZH_SIZE * Y_SIZE
    n_col = lax.axis_size("col")
    n_xy = X_SIZE * Y_SIZE
    xy_groups = [
        [(x * ZH_SIZE + zh) * Y_SIZE + y for x in range(X_SIZE) for y in range(Y_SIZE)]
        for zh in range(ZH_SIZE)
    ]
    zh_swap = [
        ((x * ZH_SIZE + zh) * Y_SIZE + y, (x * ZH_SIZE + 1 - zh) * Y_SIZE + y)
        for x in range(X_SIZE)
        for zh in range(ZH_SIZE)
        for y in range(Y_SIZE)
    ]

    moved_pos = positions + TIME_STEP * vel_half
    centred = (moved_pos - CENTRE).reshape(3, tiles_dev, TILE_ATOMS)
    square = centred[0] * centred[0] + centred[1] * centred[1] + centred[2] * centred[2]
    block = jnp.stack(
        [
            centred[0],
            centred[1],
            centred[2],
            square,
            jnp.ones_like(square),
            charges.reshape(tiles_dev, TILE_ATOMS),
            types.astype(jnp.float32).reshape(tiles_dev, TILE_ATOMS),
            jnp.zeros_like(square),
        ],
        axis=1,
    )
    pad = ((0, TYPE_ROWS - BEAD_TYPES), (0, TYPE_ROWS - BEAD_TYPES))
    six = jnp.pad(six_table.T * (6.0 / CUT_SQ**2), pad)
    twelve = jnp.pad(twelve_table.T * (12.0 / CUT_SQ**2), pad)
    parts = []
    for table in (six, twelve):
        upper = lax.reduce_precision(table, 8, 7)
        parts += [upper, table - upper]
    tables = jnp.concatenate(parts, axis=0).astype(jnp.bfloat16)

    rows_dev = tiles_dev * 8
    block = block.reshape(rows_dev, LANES)
    far_block = lax.ppermute(block, "row", zh_swap)
    row_blocks = lax.all_to_all(
        jnp.broadcast_to(block[None], (n_col, rows_dev, LANES)), "col", 0, 0
    )
    both = jnp.concatenate([block, far_block], axis=0)
    col_blocks = lax.all_to_all(
        jnp.broadcast_to(both[None], (n_xy, 2 * rows_dev, LANES)),
        "row",
        0,
        0,
        axis_index_groups=xy_groups,
    )
    row_tiles = n_col * tiles_dev
    col_tiles = n_row * tiles_dev
    smem = pl.BlockSpec(memory_space=pltpu.SMEM)
    vmem = pl.BlockSpec(memory_space=pltpu.VMEM)
    row_force, col_force = pl.pallas_call(
        pair_kernel,
        out_shape=(
            jax.ShapeDtypeStruct((row_tiles, 4, LANES), jnp.float32),
            jax.ShapeDtypeStruct((col_tiles, 4, LANES), jnp.float32),
        ),
        in_specs=[smem, smem, vmem, vmem, vmem],
        out_specs=(vmem, vmem),
        scratch_shapes=[pltpu.VMEM((row_tiles, 4 * TILE_ATOMS, LANES), jnp.bfloat16)],
        compiler_params=pltpu.CompilerParams(vmem_limit_bytes=32 * 2**20),
        name="pair_forces",
    )(
        tile_pairs,
        pair_counts,
        row_blocks.reshape(row_tiles, 8, LANES),
        col_blocks.reshape(col_tiles, 8, LANES),
        tables,
    )
    col_parts = lax.all_to_all(
        col_force.reshape(n_xy, ZH_SIZE * tiles_dev * 4, LANES),
        "row",
        0,
        0,
        axis_index_groups=xy_groups,
    )
    col_sum = jnp.sum(col_parts, axis=0)
    half = tiles_dev * 4
    far_sum = lax.ppermute(col_sum[half:], "row", zh_swap)
    row_parts = lax.all_to_all(
        row_force.reshape(n_col, tiles_dev * 4, LANES), "col", 0, 0
    )
    force = jnp.sum(row_parts, axis=0) + col_sum[:half] + far_sum
    force_new = force.reshape(tiles_dev, 4, TILE_ATOMS)[:, 0:3].transpose(1, 0, 2)
    force_new = force_new.reshape(3, atoms_dev)
    velocity_new = vel_half + HALF_KICK * force_new
    return (moved_pos, force_new, velocity_new)


def solution(mesh):
    placed = (
        P(None, ("row", "col")),
        P(None, ("row", "col")),
        P(("row", "col")),
        P(("row", "col")),
        P(),
        P(),
        P("row", "col", None, None),
        P("row", "col"),
    )
    return jax.shard_map(
        shards,
        mesh=mesh,
        in_specs=placed,
        out_specs=(P(None, ("row", "col")), P(None, ("row", "col")), P(None, ("row", "col"))),
        check_vma=False,
    )
```

time: 1110 us -> 156 us (0.14)
  the two profiles are of different devices: /device:TPU:8 before, /device:TPU:1 now
where the time goes in v1:
time: 156 us; the launch traced here: 155 us
  blocking collectives  47.4 us (30%)
  starting transfers between devices  43.2 us (28%)
  Pallas kernels  36 us (23%)
  waiting for transfers between devices  21.3 us (14%)
  local copies, waits for them, and re-layouts  3.65 us (2%)
  other arithmetic  2.09 us (1%)
    pallas_call x1, Pallas kernels, shards(): pl.pallas_call(pair_kernel, out_shape=(jax.ShapeDtypeStruct((row_tiles, 4...  36 us
    all_to_all x1, blocking collectives, shards(): lax.all_to_all(col_force.reshape(n_xy, ZH_SIZE * tiles_dev * 4, LANES), '...  31.7 us
    ppermute x1, starting transfers between devices, shards(): far_block = lax.ppermute(block, 'row', zh_swap)  16.3 us
    all_to_all x1, blocking collectives, shards(): lax.all_to_all(jnp.broadcast_to(both[None], (n_xy, 2 * rows_dev, LANES)),...  15.7 us
    all_to_all x1, waiting for transfers between devices, shards(): lax.all_to_all(jnp.broadcast_to(block[None], (n_col, rows_dev, LANES)), '...  15.4 us
    all_to_all x1, starting transfers between devices, shards(): lax.all_to_all(jnp.broadcast_to(block[None], (n_col, rows_dev, LANES)), '...  12.5 us
    ppermute x1, starting transfers between devices, shards(): far_sum = lax.ppermute(col_sum[half:], 'row', zh_swap)  8.46 us
    all_to_all x1, starting transfers between devices, shards(): lax.all_to_all(row_force.reshape(n_col, tiles_dev * 4, LANES), 'col', 0, 0)  5.93 us
  transfers between devices with their start and end apart: 4, of which 4 were waited for; matrix products, arithmetic and copies ran while one was open for 0% of the time, Pallas kernels for 0%

profile of v1, /device:TPU:1, one launch (start us, length us, event | category | flops | bytes accessed | tf_op | source)
XLA Modules:
  0.0 154.9 jit_solution(9319194201876484470)
XLA Ops:
  0.6 1.3 broadcast_add_fusion
  2.0 0.0 copy-start.5
  2.0 0.7 copy-done.5
  2.6 0.0 copy-start.4
  2.6 0.7 copy-done.4
  3.4 16.3 %collective-permute-start = (f32[32,128]{1,0:T(8,128)S(1)}, f32[32,128]{1,0:T(8,128)S(1)}, u32[]{:S(2)}, u32[]{:S(2)}) collective-permute-start(f32[32,128]{1,0:T(8,128)S(1)} %bitcast.32), channel_id=1, source_target_pairs={{0,64},{16,80},{32,96},{48,112},{64,0},{80,16},{96,32},{112,48},{1... | collective-permute-start | bytes 49160 | tf_op jit(solution)/shard_map/ppermute | solution.py:192
  19.6 1.2 collective-permute-done
  20.9 15.7 %all_to_all.20 = f32[16,64,128]{2,1,0:T(8,128)S(1)} all-to-all(f32[16,64,128]{2,1,0:T(8,128)S(1)} %broadcast_in_dim.15), channel_id=1, replica_groups={{0,16,32,48,128,144,160,176,256,272,288,304,384,400,416,432},{64,80,96,..., dimensions={0} | all-to-all | bytes 1048576 | tf_op jit(solution)/shard_map/all_to_all | solution.py:197
  36.6 0.7 broadcast_in_dim.14
  37.3 0.0 copy-start.2
  37.3 12.5 %all-to-all-start = ((f32[16,32,128]{2,1,0:T(8,128)}), f32[16,32,128]{2,1,0:T(8,128)S(1)}, u32[]{:S(2)}, u32[]{:S(2)}) async-start(f32[16,32,128]{2,1,0:T(8,128)} %broadcast_in_dim.14), calls=%async_computation | async-start | bytes 524288 | tf_op jit(solution)/shard_map/all_to_all | solution.py:193
  49.8 0.0 copy-done.2
  49.9 0.0 copy-start.3
  49.9 0.7 copy-done.3
  50.6 0.1 pad_maximum_fusion.1
  50.7 0.1 copy.15.table_ref
  51.4 15.4 %all-to-all-done = f32[16,32,128]{2,1,0:T(8,128)S(1)} async-done(((f32[16,32,128]{2,1,0:T(8,128)}), f32[16,32,128]{2,1,0:T(8,128)S(1)}, u32[]{:S(2)}, u32[]{:S(2)}) %all-to-all-start) | async-done | bytes 262176 | tf_op jit(solution)/shard_map/all_to_all | solution.py:193
  66.8 0.0 copy-start
  66.9 0.7 copy-done
  67.5 36.0 %pair_forces.1 = (f32[64,4,128]{2,1,0:T(4,128)}, f32[128,4,128]{2,1,0:T(4,128)S(1)}) custom-call(s32[1,1,2,128]{3,2,1,0:T(2,128)S(1)} %copy-done, s32[1,1]{1,0:T(1,128)S(6)} %copy.16.count_ref, f32[64,8,128]{2,1,0:T(8,128)S(1)} %bitcast.30, f32[128,8,128]{2,1,0:T(8,128)S(1)} %bitcast.29, bf16[96,24]{1,0:T(8,128)(2,1)S(1)} %copy.15.table_ref), custom_call_target="tpu_custom_call" | custom-call | tf_op jit(solution)/shard_map/pair_forces/pallas_call | solution.py:208
  103.5 31.7 %all_to_all.21 = f32[16,32,128]{2,1,0:T(8,128)S(1)} all-to-all(f32[16,32,128]{2,1,0:T(8,128)S(1)} %bitcast.31), channel_id=1, replica_groups={{0,16,32,48,128,144,160,176,256,272,288,304,384,400,416,432},{64,80,96,..., dimensions={0} | all-to-all | bytes 524288 | tf_op jit(solution)/shard_map/all_to_all | solution.py:226
  135.2 5.9 %all-to-all-start.2 = ((f32[16,16,128]{2,1,0:T(8,128)}), f32[16,16,128]{2,1,0:T(8,128)S(1)}, u32[]{:S(2)}, u32[]{:S(2)}) async-start(f32[16,16,128]{2,1,0:T(8,128)} %bitcast.10), calls=%async_computation.2 | async-start | bytes 262144 | tf_op jit(solution)/shard_map/all_to_all | solution.py:236
  141.1 8.5 %collective-permute-start.1 = (f32[16,128]{1,0:T(8,128)S(1)}, f32[16,128]{1,0:T(8,128)S(1)}, u32[]{:S(2)}, u32[]{:S(2)}) collective-permute-start(f32[16,128]{1,0:T(8,128)S(1)} %slice.37), channel_id=1, source_target_pairs={{0,64},{16,80},{32,96},{48,112},{64,0},{80,16},{96,32},{112,48},{1... | collective-permute-start | bytes 24584 | tf_op jit(solution)/shard_map/ppermute | solution.py:235
  149.6 3.6 %all-to-all-done.2 = f32[16,16,128]{2,1,0:T(8,128)S(1)} async-done(((f32[16,16,128]{2,1,0:T(8,128)}), f32[16,16,128]{2,1,0:T(8,128)S(1)}, u32[]{:S(2)}, u32[]{:S(2)}) %all-to-all-start.2) | async-done | bytes 131104 | tf_op jit(solution)/shard_map/all_to_all | solution.py:236
  153.2 0.0 copy-start.1
  153.2 1.0 collective-permute-done.1
  154.3 0.0 copy-done.1
  154.3 0.6 multiply_add_fusion
  (15 shorter events, 0.2 us)
Async XLA Ops:
  2.0 0.7 copy-start.5
  2.6 0.7 copy-start.4
  3.4 17.5 %collective-permute-start = (f32[32,128]{1,0:T(8,128)S(1)}, f32[32,128]{1,0:T(8,128)S(1)}, u32[]{:S(2)}, u32[]{:S(2)}) collective-permute-start(f32[32,128]{1,0:T(8,128)S(1)} %bitcast.32), channel_id=1, source_target_pairs={{0,64},{16,80},{32,96},{48,112},{64,0},{80,16},{96,32},{112,48},{1... | collective-permute-start | bytes 49160 | tf_op jit(solution)/shard_map/ppermute | solution.py:192
  37.3 12.5 %copy-start.2 = (f32[18,18]{1,0:T(8,128)S(1)}, f32[18,18]{1,0:T(8,128)}, u32[]{:S(2)}) copy-start(f32[18,18]{1,0:T(8,128)} %param.13) | copy-start | bytes 3892
  37.3 29.5 %all-to-all-start = ((f32[16,32,128]{2,1,0:T(8,128)}), f32[16,32,128]{2,1,0:T(8,128)S(1)}, u32[]{:S(2)}, u32[]{:S(2)}) async-start(f32[16,32,128]{2,1,0:T(8,128)} %broadcast_in_dim.14), calls=%async_computation | async-start | bytes 524288 | tf_op jit(solution)/shard_map/all_to_all | solution.py:193
  49.9 0.7 copy-start.3
  66.8 0.7 copy-start
  135.2 18.0 %all-to-all-start.2 = ((f32[16,16,128]{2,1,0:T(8,128)}), f32[16,16,128]{2,1,0:T(8,128)S(1)}, u32[]{:S(2)}, u32[]{:S(2)}) async-start(f32[16,16,128]{2,1,0:T(8,128)} %bitcast.10), calls=%async_computation.2 | async-start | bytes 262144 | tf_op jit(solution)/shard_map/all_to_all | solution.py:236
  141.1 13.1 %collective-permute-start.1 = (f32[16,128]{1,0:T(8,128)S(1)}, f32[16,128]{1,0:T(8,128)S(1)}, u32[]{:S(2)}, u32[]{:S(2)}) collective-permute-start(f32[16,128]{1,0:T(8,128)S(1)} %slice.37), channel_id=1, source_target_pairs={{0,64},{16,80},{32,96},{48,112},{64,0},{80,16},{96,32},{112,48},{1... | collective-permute-start | bytes 24584 | tf_op jit(solution)/shard_map/ppermute | solution.py:235
  153.2 1.0 copy-start.1

commit v2 on v1

v2 whole, which is shorter than its diff:
```python
import functools
import jax
import jax.numpy as jnp
from jax import lax
from jax.experimental import pallas as pl
from jax.experimental.pallas import tpu as pltpu
from jax.sharding import PartitionSpec as P

TILE_ATOMS = 128
TILES_DEV = 4
BEAD_TYPES = 18
LANES = 128

TIME_STEP = 0.02
HALF_KICK = 0.01 / 72.0
SOFT_CORE = 0.5
COULOMB = 9.262364
REACTION = 0.28935185
CUT_SQ = 1.44
CENTRE = 1.2

X_SIZE = 4
ZH_SIZE = 2
Y_SIZE = 4
N_COL = 16
CORES = 2
CHANNELS = 6
TYPE_ROWS = 24
UNROLL = 16
PREPARED = 4

def split_three(values):
    upper = values.astype(jnp.bfloat16).astype(jnp.float32)
    rest = values - upper
    middle = rest.astype(jnp.bfloat16).astype(jnp.float32)
    return upper, middle, rest - middle


def pair_kernel(
    pairs_ref, count_ref, own_ref, other_ref, col_ref, table_ref,
    own_force, other_force, col_force,
    row_block, col_block, row_sum, col_sum, lhs_ref, scalar_ref
):
    tiles_dev = TILES_DEV
    my_row = lax.axis_index("row")
    my_col = lax.axis_index("col")
    my_zh = (my_row // Y_SIZE) % ZH_SIZE
    my_core = my_col % CORES
    half_tiles = row_block.shape[0] // CORES
    f32 = jnp.float32
    bf16 = jnp.bfloat16
    sub8 = lax.broadcasted_iota(jnp.int32, (8, LANES), 0)
    type_rows = lax.broadcasted_iota(jnp.int32, (TYPE_ROWS, LANES), 0).astype(f32)
    lane = lax.broadcasted_iota(jnp.int32, (TILE_ATOMS, LANES), 1)
    is_charge = (lane % 8 == 4) & (lane < 32)
    is_dist = (lane % 8 != 4) & (lane < 32)
    is_six = (lane >= 32) & (lane < 80)
    is_twelve = lane >= 80
    scale = jnp.where(sub8 < 3, -2.0, jnp.where(sub8 == 4, COULOMB / CUT_SQ**2, 0.0)).astype(f32)
    one_zero = jnp.where(lax.broadcasted_iota(jnp.int32, (2, LANES), 0) == 0, 1.0, 0.0).astype(f32)

    row_sum[...] = jnp.zeros(row_sum.shape, f32)
    col_sum[...] = jnp.zeros(col_sum.shape, f32)
    scalar_ref[...] = jnp.zeros(scalar_ref.shape, bf16)

    def hot_types(block):
        return (jnp.broadcast_to(block[5:6], (TYPE_ROWS, LANES)) == type_rows).astype(f32)

    def spread(source, owner, target, start):
        rows = source[owner]
        for tile in range(tiles_dev):
            piece = rows[CHANNELS * tile : CHANNELS * (tile + 1)]
            target[start + owner * tiles_dev + tile] = jnp.concatenate([piece, one_zero], axis=0)

    def spread_owners(index, carry):
        spread(own_ref, index, row_block, 0)
        spread(other_ref, index, row_block, half_tiles)
        for part in range(4):
            spread(col_ref, index * 4 + part, col_block, 0)
        return carry

    lax.fori_loop(0, own_ref.shape[0], spread_owners, 0)

    def prepare(index, carry):
        wholes = []
        for part in range(PREPARED):
            block = row_block[index * PREPARED + part]
            left = block * scale
            left = jnp.where(sub8 == 3, 1.0, left)
            left = jnp.where(sub8 == 6, block[3:4] + SOFT_CORE, left)
            upper, middle, _ = split_three(left)
            coefs = jnp.dot(
                table_ref[...], hot_types(block).astype(bf16), preferred_element_type=f32
            )
            wholes.append(jnp.concatenate([upper, upper, middle, middle, coefs], axis=0))
        for part in range(PREPARED):
            whole = wholes[part].T
            for which, keep in enumerate((is_dist, is_charge, is_six, is_twelve)):
                lhs_ref[
                    index * PREPARED + part, which * TILE_ATOMS : (which + 1) * TILE_ATOMS, :
                ] = jnp.where(keep, whole, 0.0).astype(bf16)
        return carry

    lax.fori_loop(0, row_block.shape[0] // PREPARED, prepare, 0)

    def features(first, place):
        right = col_block[place]
        upper, middle, _ = split_three(right)
        hot = hot_types(right)
        rhs = jnp.concatenate([upper, middle, upper, middle, hot, hot, hot, hot], axis=0)
        return jnp.dot(lhs_ref[first], rhs.astype(bf16), preferred_element_type=f32)

    def scalars(looked, same, part):
        soft_sq = looked[0:128]
        charge = looked[128:256]
        six = looked[256:384]
        twelve = looked[384:512]
        root = lax.rsqrt(soft_sq)
        inverse = root * root
        inverse_two = inverse * inverse
        inverse_four = inverse_two * inverse_two
        dispersion = inverse_four * (twelve * (inverse_two * inverse) - six)
        coulomb = charge * (inverse * root - 2.0 * REACTION)
        switch = jnp.maximum((CUT_SQ + SOFT_CORE) - soft_sq, 0.0)
        scalar = (dispersion + coulomb) * (switch * switch)
        if same is not None:
            at_i = lax.broadcasted_iota(jnp.int32, (TILE_ATOMS, LANES), 0)
            scalar = jnp.where((at_i < lane) | jnp.logical_not(same), scalar, 0.0)
        high = scalar.astype(bf16)
        scalar_ref[part, 0] = high
        scalar_ref[part, 1] = (scalar - high.astype(f32)).astype(bf16)

    def add_forces(first, place, part):
        left = row_block[first]
        right = col_block[place]
        left_x = jnp.concatenate([*split_three(left), jnp.zeros_like(left)], axis=0).astype(bf16)
        right_x = jnp.concatenate([*split_three(right), jnp.zeros_like(right)], axis=0).astype(bf16)
        high = scalar_ref[part, 0]
        low = scalar_ref[part, 1]
        sums_i = lax.dot_general(
            jnp.concatenate([right_x, right_x], axis=1),
            jnp.concatenate([high, low], axis=1),
            (((1,), (1,)), ((), ())),
            preferred_element_type=f32,
        )
        sums_j = jnp.dot(
            jnp.concatenate([left_x, left_x], axis=1),
            jnp.concatenate([high, low], axis=0),
            preferred_element_type=f32,
        )
        sums_i = sums_i[0:8] + sums_i[8:16] + sums_i[16:24]
        sums_j = sums_j[0:8] + sums_j[8:16] + sums_j[16:24]
        row_sum[first] += left * sums_i[6:7] - sums_i
        col_sum[place] += right * sums_j[6:7] - sums_j

    def find(slot):
        first = pairs_ref[0, 0, 0, slot]
        second = pairs_ref[0, 0, 1, slot]
        owner = second >> 2
        tile = second & 3
        same = (owner == my_row) & (first == my_col * tiles_dev + tile)
        far = ((owner >> 2) & 1) ^ my_zh
        place = ((owner & 24) << 2) | ((owner & 3) << 3) | (far << 2) | tile
        owner = first >> 2
        first = (((owner & 1) ^ my_core) << 5) | ((owner >> 1) << 2) | (first & 3)
        return first, place, same

    def step(index, before):
        found = [find(index * UNROLL + part) for part in range(UNROLL)]
        any_same = functools.reduce(jnp.logical_or, [same for _, _, same in found])

        def work(masked):
            looked = []
            for part, (first, place, _) in enumerate(found):
                looked.append(features(first, place))
                add_forces(before[2 * part], before[2 * part + 1], part)
            for part, (_, _, same) in enumerate(found):
                scalars(looked[part], same if masked else None, part)

        @pl.when(any_same)
        def _():
            work(True)

        @pl.when(jnp.logical_not(any_same))
        def _():
            work(False)

        return tuple(place for first, second, _ in found for place in (first, second))

    last = lax.fori_loop(
        0, count_ref[0, 0] // UNROLL, step, tuple(jnp.int32(0) for _ in range(2 * UNROLL))
    )
    for part in range(UNROLL):
        add_forces(last[2 * part], last[2 * part + 1], part)
    own_force[...] = row_sum[0:half_tiles, 0:4, :]
    other_force[...] = row_sum[half_tiles:, 0:4, :]
    col_force[...] = col_sum[:, 0:4, :]


def shards(positions, vel_half, charges, types, six_table, twelve_table, tile_pairs, pair_counts):
    atoms_dev = positions.shape[1]
    tiles_dev = TILES_DEV
    n_row = X_SIZE * ZH_SIZE * Y_SIZE
    n_col = N_COL
    n_xy = X_SIZE * Y_SIZE
    n_zl = n_col // CORES
    n_z = ZH_SIZE * n_zl
    my_zh = (lax.axis_index("row") // Y_SIZE) % ZH_SIZE
    my_zl = lax.axis_index("col") // CORES
    xy_groups = [
        [(x * ZH_SIZE + zh) * Y_SIZE + y for x in range(X_SIZE) for y in range(Y_SIZE)]
        for zh in range(ZH_SIZE)
    ]
    z_groups = [
        [
            ((x * ZH_SIZE + zh) * Y_SIZE + y) * n_col + zl * CORES + core
            for zh in range(ZH_SIZE)
            for zl in range(n_zl)
        ]
        for x in range(X_SIZE)
        for y in range(Y_SIZE)
        for core in range(CORES)
    ]
    zl_groups = [list(range(core, n_col, CORES)) for core in range(CORES)]
    core_swap = [(at, at ^ 1) for at in range(n_col)]
    zh_swap = [(at, at ^ Y_SIZE) for at in range(n_row)]

    moved_pos = positions + TIME_STEP * vel_half
    centred = (moved_pos - CENTRE).reshape(3, tiles_dev, TILE_ATOMS)
    square = centred[0] * centred[0] + centred[1] * centred[1] + centred[2] * centred[2]
    block = jnp.stack(
        [
            centred[0],
            centred[1],
            centred[2],
            square,
            charges.reshape(tiles_dev, TILE_ATOMS),
            types.astype(jnp.float32).reshape(tiles_dev, TILE_ATOMS),
        ],
        axis=1,
    )
    pad = ((0, TYPE_ROWS - BEAD_TYPES), (0, TYPE_ROWS - BEAD_TYPES))
    six = jnp.pad(six_table.T * (6.0 / CUT_SQ**2), pad)
    twelve = jnp.pad(twelve_table.T * (12.0 / CUT_SQ**2), pad)
    parts = []
    for table in (six, twelve):
        upper = lax.reduce_precision(table, 8, 7)
        parts += [upper, table - upper]
    tables = jnp.concatenate(parts, axis=0).astype(jnp.bfloat16)

    rows_dev = tiles_dev * CHANNELS
    block = block.reshape(rows_dev, LANES)
    far_block = lax.ppermute(block, "row", zh_swap)
    own_blocks = lax.all_to_all(
        jnp.broadcast_to(block[None], (n_zl, rows_dev, LANES)),
        "col",
        0,
        0,
        axis_index_groups=zl_groups,
    )
    far_block, own_blocks = lax.optimization_barrier((far_block, own_blocks))
    other_blocks = lax.ppermute(own_blocks, "col", core_swap)
    both = jnp.stack([block, far_block], axis=0)
    col_blocks = lax.all_to_all(
        jnp.broadcast_to(both[None], (n_xy, ZH_SIZE, rows_dev, LANES)),
        "row",
        0,
        0,
        axis_index_groups=xy_groups,
    )
    row_tiles = n_col * tiles_dev
    col_tiles = n_row * tiles_dev
    smem = pl.BlockSpec(memory_space=pltpu.SMEM)
    vmem = pl.BlockSpec(memory_space=pltpu.VMEM)
    own_force, other_force, col_force = pl.pallas_call(
        pair_kernel,
        out_shape=(
            jax.ShapeDtypeStruct((row_tiles // CORES, 4, LANES), jnp.float32),
            jax.ShapeDtypeStruct((row_tiles // CORES, 4, LANES), jnp.float32),
            jax.ShapeDtypeStruct((col_tiles, 4, LANES), jnp.float32),
        ),
        in_specs=[smem, smem, vmem, vmem, vmem, vmem],
        out_specs=(vmem, vmem, vmem),
        scratch_shapes=[
            pltpu.VMEM((row_tiles, 8, LANES), jnp.float32),
            pltpu.VMEM((col_tiles, 8, LANES), jnp.float32),
            pltpu.VMEM((row_tiles, 8, LANES), jnp.float32),
            pltpu.VMEM((col_tiles, 8, LANES), jnp.float32),
            pltpu.VMEM((row_tiles, 4 * TILE_ATOMS, LANES), jnp.bfloat16),
            pltpu.VMEM((UNROLL, 2, TILE_ATOMS, LANES), jnp.bfloat16),
        ],
        compiler_params=pltpu.CompilerParams(vmem_limit_bytes=32 * 2**20),
        name="pair_forces",
    )(
        tile_pairs,
        pair_counts,
        own_blocks,
        other_blocks,
        col_blocks.reshape(n_row, rows_dev, LANES),
        tables,
    )
    core_force = lax.ppermute(other_force, "col", core_swap)
    col_parts = lax.all_to_all(
        col_force.reshape(n_xy, ZH_SIZE * tiles_dev * 4, LANES),
        "row",
        0,
        0,
        axis_index_groups=xy_groups,
    )
    col_sum = jnp.sum(col_parts, axis=0)
    half = tiles_dev * 4
    row_sum = (own_force + core_force).reshape(1, n_zl, half, LANES)
    to_zh = lax.broadcasted_iota(jnp.int32, (ZH_SIZE, n_zl, half, LANES), 0)
    to_zl = lax.broadcasted_iota(jnp.int32, (ZH_SIZE, n_zl, half, LANES), 1)
    far_sum = jnp.where(to_zl == my_zl, col_sum[half:][None, None], 0.0)
    z_parts = lax.all_to_all(
        jnp.where(to_zh == my_zh, row_sum, far_sum).reshape(n_z, half, LANES),
        ("row", "col"),
        0,
        0,
        axis_index_groups=z_groups,
    )
    force = jnp.sum(z_parts, axis=0) + col_sum[:half]
    force_new = force.reshape(tiles_dev, 4, TILE_ATOMS)[:, 0:3].transpose(1, 0, 2)
    force_new = force_new.reshape(3, atoms_dev)
    velocity_new = vel_half + HALF_KICK * force_new
    return (moved_pos, force_new, velocity_new)


def solution(mesh):
    placed = (
        P(None, ("row", "col")),
        P(None, ("row", "col")),
        P(("row", "col")),
        P(("row", "col")),
        P(),
        P(),
        P("row", "col", None, None),
        P("row", "col"),
    )
    return jax.shard_map(
        shards,
        mesh=mesh,
        in_specs=placed,
        out_specs=(P(None, ("row", "col")), P(None, ("row", "col")), P(None, ("row", "col"))),
        check_vma=False,
    )
```

time: 156 us -> 101 us (0.65)
  the two profiles are of different devices: /device:TPU:1 before, /device:TPU:32 now
where the time goes in v2:
time: 101 us
  starting transfers between devices  40.3 us (40%)
  blocking collectives  22.6 us (22%)
  waiting for transfers between devices  18.6 us (18%)
  Pallas kernels  11.5 us (11%)
  local copies, waits for them, and re-layouts  3.85 us (4%)
  other arithmetic  2.23 us (2%)
  between operations  1.5 us (1%)
    all_to_all x1, blocking collectives, shards(): lax.all_to_all(jnp.where(to_zh == my_zh, row_sum, far_sum).reshape(n_z, h...  22.6 us
    all_to_all x1, starting transfers between devices, shards(): lax.all_to_all(jnp.broadcast_to(block[None], (n_zl, rows_dev, LANES)), 'c...  12.8 us
    pallas_call x1, Pallas kernels, shards(): pl.pallas_call(pair_kernel, out_shape=(jax.ShapeDtypeStruct((row_tiles //...  11.5 us
    all_to_all x1, starting transfers between devices, shards(): lax.all_to_all(col_force.reshape(n_xy, ZH_SIZE * tiles_dev * 4, LANES), '...  8.35 us
    ppermute x1, starting transfers between devices, shards(): far_block = lax.ppermute(block, 'row', zh_swap)  8.21 us
    all_to_all x1, starting transfers between devices, shards(): lax.all_to_all(jnp.broadcast_to(both[None], (n_xy, ZH_SIZE, rows_dev, LAN...  7.17 us
    all_to_all x1, waiting for transfers between devices, shards(): lax.all_to_all(jnp.broadcast_to(both[None], (n_xy, ZH_SIZE, rows_dev, LAN...  5.89 us
    ppermute x1, waiting for transfers between devices, shards(): far_block = lax.ppermute(block, 'row', zh_swap)  5.4 us
  transfers between devices with their start and end apart: 6, of which 5 were waited for; matrix products, arithmetic and copies ran while one was open for 0% of the time, Pallas kernels for 0%

profile of v2, /device:TPU:32, one launch (start us, length us, event | category | flops | bytes accessed | tf_op | source)
XLA Modules:
  0.0 100.6 jit_solution(12342191729603299187)
XLA Ops:
  0.6 1.3 %broadcast_add_fusion = (f32[3,512]{1,0:T(4,128)S(1)}, f32[3,512]{1,0:T(4,128)}) fusion(f32[3,512]{1,0:T(4,128)} %param.8, f32[3,512]{1,0:T(4,128)} %param.9), kind=kLoop, calls=%fused_computation.21 | loop fusion | flops 4608 | bytes 24576 | tf_op jit(solution)/shard_map/sub | solution.py:229
  2.0 0.0 copy-start.4
  2.0 0.7 copy-done.4
  2.7 0.0 copy-start.5
  2.7 0.7 copy-done.5
  3.4 0.6 broadcast_in_dim.36
  4.0 0.0 copy-start.2
  4.0 12.8 %all-to-all-start = ((f32[8,24,128]{2,1,0:T(8,128)}), f32[8,24,128]{2,1,0:T(8,128)S(1)}, u32[]{:S(2)}, u32[]{:S(2)}) async-start(f32[8,24,128]{2,1,0:T(8,128)} %broadcast_in_dim.36), calls=%async_computation | async-start | bytes 196608 | tf_op jit(solution)/shard_map/all_to_all | solution.py:254
  16.8 8.2 %collective-permute-start = (f32[24,128]{1,0:T(8,128)S(1)}, f32[24,128]{1,0:T(8,128)S(1)}, u32[]{:S(2)}, u32[]{:S(2)}) collective-permute-start(f32[24,128]{1,0:T(8,128)S(1)} %reshape.76), channel_id=1, source_target_pairs={{0,64},{16,80},{32,96},{48,112},{64,0},{80,16},{96,32},{112,48},{1... | collective-permute-start | bytes 36872 | tf_op jit(solution)/shard_map/ppermute | solution.py:253
  25.0 0.0 copy-done.2
  25.7 5.4 %collective-permute-done = f32[24,128]{1,0:T(8,128)S(1)} collective-permute-done((f32[24,128]{1,0:T(8,128)S(1)}, f32[24,128]{1,0:T(8,128)S(1)}, u32[]{:S(2)}, u32[]{:S(2)}) %collective-permute-start) | collective-permute-done | bytes 12320 | tf_op jit(solution)/shard_map/ppermute | solution.py:253
  31.1 0.0 all-to-all-done.own_ref
  31.1 0.8 broadcast_in_dim.37
  31.8 0.0 copy-start.3
  31.8 7.2 %all-to-all-start.1 = ((f32[16,2,24,128]{3,2,1,0:T(8,128)}), f32[16,2,24,128]{3,2,1,0:T(8,128)S(1)}, u32[]{:S(2)}, u32[]{:S(2)}) async-start(f32[16,2,24,128]{3,2,1,0:T(8,128)} %broadcast_in_dim.37), calls=%async_computation.1 | async-start | bytes 786432 | tf_op jit(solution)/shard_map/all_to_all | solution.py:264
  39.0 0.0 copy-done.3
  39.1 1.9 %collective-permute-start.1 = (f32[8,24,128]{2,1,0:T(8,128)S(1)}, f32[8,24,128]{2,1,0:T(8,128)S(1)}, u32[]{:S(2)}, u32[]{:S(2)}) collective-permute-start(f32[8,24,128]{2,1,0:T(8,128)S(1)} %all-to-all-done.own_ref), channel_id=1, source_target_pairs={{0,1},{1,0},{2,3},{3,2},{4,5},{5,4},{6,7},{7,6},{8,9},{9,8},{10,11... | collective-permute-start | bytes 294920 | tf_op jit(solution)/shard_map/ppermute | solution.py:262
  41.0 0.1 pad_maximum_fusion.1
  41.1 0.1 copy.48.table_ref
  41.2 0.0 copy-start
  41.2 1.1 %collective-permute-done.1.other_ref = f32[8,24,128]{2,1,0:T(8,128)S(1)} collective-permute-done((f32[8,24,128]{2,1,0:T(8,128)S(1)}, f32[8,24,128]{2,1,0:T(8,128)S(1)}, u32[]{:S(2)}, u32[]{:S(2)}) %collective-permute-start.1) | collective-permute-done | bytes 98336 | tf_op jit(solution)/shard_map/ppermute | solution.py:262
  42.3 5.9 %all-to-all-done.1 = f32[16,2,24,128]{3,2,1,0:T(8,128)S(1)} async-done(((f32[16,2,24,128]{3,2,1,0:T(8,128)}), f32[16,2,24,128]{3,2,1,0:T(8,128)S(1)}, u32[]{:S(2)}, u32[]{:S(2)}) %all-to-all-start.1) | async-done | bytes 393248 | tf_op jit(solution)/shard_map/all_to_all | solution.py:264
  48.2 0.0 copy-done
  48.2 11.5 %pair_forces.1 = (f32[32,4,128]{2,1,0:T(4,128)S(1)}, f32[32,4,128]{2,1,0:T(4,128)S(1)}, f32[128,4,128]{2,1,0:T(4,128)}) custom-call(s32[1,1,2,128]{3,2,1,0:T(2,128)S(1)} %copy-done, s32[1,1]{1,0:T(1,128)S(6)} %copy.54.count_ref, f32[8,24,128]{2,1,0:T(8,128)S(1)} %all-to-all-done.own_ref, f32[8,24,128]{2,1,0:T(8,128)S(1)} %collective-permute-done.1.other_ref, ...), custom_call_target="tpu_custom_call" | custom-call | tf_op jit(solution)/shard_map/pair_forces/pallas_call | solution.py:275
  59.7 8.3 %all-to-all-start.2 = ((f32[16,32,128]{2,1,0:T(8,128)}), f32[16,32,128]{2,1,0:T(8,128)S(1)}, u32[]{:S(2)}, u32[]{:S(2)}) async-start(f32[16,32,128]{2,1,0:T(8,128)} %bitcast.11), calls=%async_computation.2 | async-start | bytes 524288 | tf_op jit(solution)/shard_map/all_to_all | solution.py:303
  68.1 0.1 iota.26
  68.2 1.9 %collective-permute-start.2 = (f32[32,4,128]{2,1,0:T(4,128)S(1)}, f32[32,4,128]{2,1,0:T(4,128)S(1)}, u32[]{:S(2)}, u32[]{:S(2)}) collective-permute-start(f32[32,4,128]{2,1,0:T(4,128)S(1)} %get-tuple-element.11), channel_id=1, source_target_pairs={{0,1},{1,0},{2,3},{3,2},{4,5},{5,4},{6,7},{7,6},{8,9},{9,8},{10,11... | collective-permute-start | bytes 196616 | tf_op jit(solution)/shard_map/ppermute | solution.py:302
  70.1 0.1 iota.21
  70.2 0.1 iota.22
  70.3 1.0 %collective-permute-done.2 = f32[32,4,128]{2,1,0:T(4,128)S(1)} collective-permute-done((f32[32,4,128]{2,1,0:T(4,128)S(1)}, f32[32,4,128]{2,1,0:T(4,128)S(1)}, u32[]{:S(2)}, u32[]{:S(2)}) %collective-permute-start.2) | collective-permute-done | bytes 65568 | tf_op jit(solution)/shard_map/ppermute | solution.py:302
  71.3 5.2 %all-to-all-done.2 = f32[16,32,128]{2,1,0:T(8,128)S(1)} async-done(((f32[16,32,128]{2,1,0:T(8,128)}), f32[16,32,128]{2,1,0:T(8,128)S(1)}, u32[]{:S(2)}, u32[]{:S(2)}) %all-to-all-start.2) | async-done | bytes 262176 | tf_op jit(solution)/shard_map/all_to_all | solution.py:303
  76.5 0.1 bitcast_select_fusion
  76.6 22.6 %all_to_all.20 = f32[16,16,128]{2,1,0:T(8,128)S(1)} all-to-all(f32[16,16,128]{2,1,0:T(8,128)S(1)} %bitcast_select_fusion), channel_id=1, replica_groups={{0,2,4,6,8,10,12,14,64,66,68,70,72,74,76,78},{1,3,5,7,9,11,13,15,65,67,..., dimensions={0} | all-to-all | bytes 262144 | tf_op jit(solution)/shard_map/all_to_all | solution.py:316
  99.3 0.0 copy-start.1
  99.3 0.7 copy-done.1
  100.0 0.6 multiply_add_fusion
  (22 shorter events, 0.2 us)
Async XLA Ops:
  2.0 0.7 copy-start.4
  2.7 0.7 copy-start.5
  4.0 21.0 %copy-start.2 = (f32[18,18]{1,0:T(8,128)S(1)}, f32[18,18]{1,0:T(8,128)}, u32[]{:S(2)}) copy-start(f32[18,18]{1,0:T(8,128)} %param.13) | copy-start | bytes 3892
  4.0 27.1 %all-to-all-start = ((f32[8,24,128]{2,1,0:T(8,128)}), f32[8,24,128]{2,1,0:T(8,128)S(1)}, u32[]{:S(2)}, u32[]{:S(2)}) async-start(f32[8,24,128]{2,1,0:T(8,128)} %broadcast_in_dim.36), calls=%async_computation | async-start | bytes 196608 | tf_op jit(solution)/shard_map/all_to_all | solution.py:254
  16.8 14.3 %collective-permute-start = (f32[24,128]{1,0:T(8,128)S(1)}, f32[24,128]{1,0:T(8,128)S(1)}, u32[]{:S(2)}, u32[]{:S(2)}) collective-permute-start(f32[24,128]{1,0:T(8,128)S(1)} %reshape.76), channel_id=1, source_target_pairs={{0,64},{16,80},{32,96},{48,112},{64,0},{80,16},{96,32},{112,48},{1... | collective-permute-start | bytes 36872 | tf_op jit(solution)/shard_map/ppermute | solution.py:253
  31.8 7.2 %copy-start.3 = (f32[18,18]{1,0:T(8,128)S(1)}, f32[18,18]{1,0:T(8,128)}, u32[]{:S(2)}) copy-start(f32[18,18]{1,0:T(8,128)} %param.12) | copy-start | bytes 3892
  31.8 16.3 %all-to-all-start.1 = ((f32[16,2,24,128]{3,2,1,0:T(8,128)}), f32[16,2,24,128]{3,2,1,0:T(8,128)S(1)}, u32[]{:S(2)}, u32[]{:S(2)}) async-start(f32[16,2,24,128]{3,2,1,0:T(8,128)} %broadcast_in_dim.37), calls=%async_computation.1 | async-start | bytes 786432 | tf_op jit(solution)/shard_map/all_to_all | solution.py:264
  39.1 3.2 %collective-permute-start.1 = (f32[8,24,128]{2,1,0:T(8,128)S(1)}, f32[8,24,128]{2,1,0:T(8,128)S(1)}, u32[]{:S(2)}, u32[]{:S(2)}) collective-permute-start(f32[8,24,128]{2,1,0:T(8,128)S(1)} %all-to-all-done.own_ref), channel_id=1, source_target_pairs={{0,1},{1,0},{2,3},{3,2},{4,5},{5,4},{6,7},{7,6},{8,9},{9,8},{10,11... | collective-permute-start | bytes 294920 | tf_op jit(solution)/shard_map/ppermute | solution.py:262
  41.2 7.0 %copy-start = (s32[1,1,2,128]{3,2,1,0:T(2,128)S(1)}, s32[1,1,2,128]{3,2,1,0:T(2,128)}, u32[]{:S(2)}) copy-start(s32[1,1,2,128]{3,2,1,0:T(2,128)} %pairs_ref.1) | copy-start | bytes 3076
  59.7 16.8 %all-to-all-start.2 = ((f32[16,32,128]{2,1,0:T(8,128)}), f32[16,32,128]{2,1,0:T(8,128)S(1)}, u32[]{:S(2)}, u32[]{:S(2)}) async-start(f32[16,32,128]{2,1,0:T(8,128)} %bitcast.11), calls=%async_computation.2 | async-start | bytes 524288 | tf_op jit(solution)/shard_map/all_to_all | solution.py:303
  68.2 3.1 %collective-permute-start.2 = (f32[32,4,128]{2,1,0:T(4,128)S(1)}, f32[32,4,128]{2,1,0:T(4,128)S(1)}, u32[]{:S(2)}, u32[]{:S(2)}) collective-permute-start(f32[32,4,128]{2,1,0:T(4,128)S(1)} %get-tuple-element.11), channel_id=1, source_target_pairs={{0,1},{1,0},{2,3},{3,2},{4,5},{5,4},{6,7},{7,6},{8,9},{9,8},{10,11... | collective-permute-start | bytes 196616 | tf_op jit(solution)/shard_map/ppermute | solution.py:302
  99.3 0.7 copy-start.1

commit v3 on v2

v3 whole, which is shorter than its diff:
```python
import functools
import jax
import jax.numpy as jnp
from jax import lax
from jax.experimental import pallas as pl
from jax.experimental.pallas import tpu as pltpu
from jax.sharding import PartitionSpec as P

TILE_ATOMS = 128
TILES_DEV = 4
BEAD_TYPES = 18
LANES = 128

TIME_STEP = 0.02
HALF_KICK = 0.01 / 72.0
SOFT_CORE = 0.5
COULOMB = 9.262364
REACTION = 0.28935185
CUT_SQ = 1.44
CENTRE = 1.2

X_SIZE = 4
ZH_SIZE = 2
Y_SIZE = 4
N_COL = 16
CORES = 2
CHANNELS = 5
TYPE_ROWS = 24
UNROLL = 16
PREPARED = 16

def split_three(values):
    upper = values.astype(jnp.bfloat16).astype(jnp.float32)
    rest = values - upper
    middle = rest.astype(jnp.bfloat16).astype(jnp.float32)
    return upper, middle, rest - middle


def pack_kernel(positions_ref, vel_ref, charge_ref, type_ref, moved_ref, block_ref, blocks_ref):
    moved = positions_ref[...] + TIME_STEP * vel_ref[...]
    moved_ref[...] = moved
    centred = moved - CENTRE
    channels = [
        jnp.concatenate(
            [
                centred[axis : axis + 1, tile * TILE_ATOMS : (tile + 1) * TILE_ATOMS]
                for tile in range(TILES_DEV)
            ],
            axis=0,
        )
        for axis in range(3)
    ]
    channels += [charge_ref[...], type_ref[...].astype(jnp.float32)]
    for channel, values in enumerate(channels):
        block_ref[channel] = values
        for copy in range(blocks_ref.shape[0]):
            blocks_ref[copy, channel] = values


def hot_types(block):
    type_rows = lax.broadcasted_iota(jnp.int32, (TYPE_ROWS, LANES), 0).astype(jnp.float32)
    return (jnp.broadcast_to(block[5:6], (TYPE_ROWS, LANES)) == type_rows).astype(jnp.float32)


def spread(source, owner, target, start):
    x, y, z, charge, kind = [source[owner, channel] for channel in range(CHANNELS)]
    one = jnp.ones_like(x)
    channels = (x, y, z, x * x + y * y + z * z, charge, kind, one, jnp.zeros_like(x))
    for channel, values in enumerate(channels):
        target[pl.ds(start, TILES_DEV), channel, :] = values


def row_kernel(own_ref, other_ref, table_ref, row_block, lhs_ref):
    f32 = jnp.float32
    half_tiles = row_block.shape[0] // CORES
    sub8 = lax.broadcasted_iota(jnp.int32, (8, LANES), 0)
    scale = jnp.where(sub8 < 3, -2.0, jnp.where(sub8 == 4, COULOMB / CUT_SQ**2, 0.0)).astype(f32)

    n_zl = own_ref.shape[0] // ZH_SIZE
    start = ((lax.axis_index("row") // Y_SIZE) % ZH_SIZE) * n_zl

    def spread_owners(index, carry):
        spread(own_ref, start + index, row_block, index * TILES_DEV)
        spread(other_ref, start + index, row_block, half_tiles + index * TILES_DEV)
        return carry

    lax.fori_loop(0, n_zl, spread_owners, 0)

    def prepare(index, carry):
        wholes = []
        for part in range(PREPARED):
            block = row_block[index * PREPARED + part]
            left = block * scale
            left = jnp.where(sub8 == 3, 1.0, left)
            left = jnp.where(sub8 == 6, block[3:4] + SOFT_CORE, left)
            upper, middle, _ = split_three(left)
            coefs = jnp.dot(
                table_ref[...],
                hot_types(block).astype(jnp.bfloat16),
                preferred_element_type=f32,
            )
            wholes.append(jnp.concatenate([upper, upper, middle, middle, coefs], axis=0))
        for part in range(PREPARED):
            lhs_ref[index * PREPARED + part] = wholes[part].T.astype(jnp.bfloat16)
        return carry

    lax.fori_loop(0, row_block.shape[0] // PREPARED, prepare, 0)


def pair_kernel(
    pairs_ref, count_ref, row_block, lhs_ref, col_ref,
    own_force, other_force, col_force,
    col_block, row_sum, col_sum, scalar_ref
):
    tiles_dev = TILES_DEV
    my_row = lax.axis_index("row")
    my_col = lax.axis_index("col")
    my_zh = (my_row // Y_SIZE) % ZH_SIZE
    my_core = my_col % CORES
    half_tiles = row_block.shape[0] // CORES
    f32 = jnp.float32
    bf16 = jnp.bfloat16
    sub8 = lax.broadcasted_iota(jnp.int32, (8, LANES), 0)
    sub8 = lax.broadcasted_iota(jnp.int32, (8, LANES), 0)
    lane = lax.broadcasted_iota(jnp.int32, (TILE_ATOMS, LANES), 1)

    row_sum[...] = jnp.zeros(row_sum.shape, f32)
    col_sum[...] = jnp.zeros(col_sum.shape, f32)
    scalar_ref[...] = jnp.zeros(scalar_ref.shape, bf16)

    def spread_owners(index, carry):
        for part in range(4):
            owner = index * 4 + part
            spread(col_ref, owner, col_block, owner * TILES_DEV)
        return carry

    lax.fori_loop(0, col_ref.shape[0] // 4, spread_owners, 0)

    def features(first, place):
        right = col_block[place]
        upper, middle, _ = split_three(right)
        hot = hot_types(right)
        zero = jnp.zeros_like(hot)
        dist = [jnp.where(sub8 == 4, 0.0, part) for part in (upper, middle)]
        charge = [jnp.where(sub8 == 4, part, 0.0) for part in (upper, middle)]
        none = jnp.zeros((32, LANES), f32)
        rhs = [
            jnp.concatenate([*dist, *dist, zero, zero, zero, zero], axis=0),
            jnp.concatenate([*charge, *charge, zero, zero, zero, zero], axis=0),
            jnp.concatenate([none, hot, hot, zero, zero], axis=0),
            jnp.concatenate([none, zero, zero, hot, hot], axis=0),
        ]
        left = lhs_ref[first]
        looked = []
        for which in (0, 2):
            both = jnp.concatenate(rhs[which : which + 2], axis=1).astype(bf16)
            product = jnp.dot(left, both, preferred_element_type=f32)
            looked += [product[:, 0:LANES], product[:, LANES:]]
        return looked

    def scalars(looked, same, part):
        soft_sq, charge, six, twelve = looked
        root = lax.rsqrt(soft_sq)
        inverse = root * root
        inverse_two = inverse * inverse
        inverse_four = inverse_two * inverse_two
        dispersion = inverse_four * (twelve * (inverse_two * inverse) - six)
        coulomb = charge * (inverse * root - 2.0 * REACTION)
        switch = jnp.maximum((CUT_SQ + SOFT_CORE) - soft_sq, 0.0)
        scalar = (dispersion + coulomb) * (switch * switch)
        if same is not None:
            at_i = lax.broadcasted_iota(jnp.int32, (TILE_ATOMS, LANES), 0)
            scalar = jnp.where((at_i < lane) | jnp.logical_not(same), scalar, 0.0)
        high = scalar.astype(bf16)
        scalar_ref[part, 0] = high
        scalar_ref[part, 1] = (scalar - high.astype(f32)).astype(bf16)

    def add_forces(first, place, part):
        left = row_block[first]
        right = col_block[place]
        left_x = jnp.concatenate([*split_three(left), jnp.zeros_like(left)], axis=0).astype(bf16)
        right_x = jnp.concatenate([*split_three(right), jnp.zeros_like(right)], axis=0).astype(bf16)
        high = scalar_ref[part, 0]
        low = scalar_ref[part, 1]
        sums_i = lax.dot_general(
            jnp.concatenate([right_x, right_x], axis=1),
            jnp.concatenate([high, low], axis=1),
            (((1,), (1,)), ((), ())),
            preferred_element_type=f32,
        )
        sums_j = jnp.dot(
            jnp.concatenate([left_x, left_x], axis=1),
            jnp.concatenate([high, low], axis=0),
            preferred_element_type=f32,
        )
        sums_i = sums_i[0:8] + sums_i[8:16] + sums_i[16:24]
        sums_j = sums_j[0:8] + sums_j[8:16] + sums_j[16:24]
        row_sum[first] += left * sums_i[6:7] - sums_i
        col_sum[place] += right * sums_j[6:7] - sums_j

    def find(slot):
        first = pairs_ref[0, 0, 0, slot]
        second = pairs_ref[0, 0, 1, slot]
        owner = second >> 2
        tile = second & 3
        same = (owner == my_row) & (first == my_col * tiles_dev + tile)
        far = ((owner >> 2) & 1) ^ my_zh
        place = ((owner & 24) << 2) | ((owner & 3) << 3) | (far << 2) | tile
        owner = first >> 2
        first = (((owner & 1) ^ my_core) << 5) | ((owner >> 1) << 2) | (first & 3)
        return first, place, same

    def step(index, before):
        found = [find(index * UNROLL + part) for part in range(UNROLL)]
        any_same = functools.reduce(jnp.logical_or, [same for _, _, same in found])

        def work(masked):
            looked = []
            for part, (first, place, _) in enumerate(found):
                looked.append(features(first, place))
                add_forces(before[2 * part], before[2 * part + 1], part)
            for part, (_, _, same) in enumerate(found):
                scalars(looked[part], same if masked else None, part)

        @pl.when(any_same)
        def _():
            work(True)

        @pl.when(jnp.logical_not(any_same))
        def _():
            work(False)

        return tuple(place for first, second, _ in found for place in (first, second))

    last = lax.fori_loop(
        0, count_ref[0, 0] // UNROLL, step, tuple(jnp.int32(0) for _ in range(2 * UNROLL))
    )
    for part in range(UNROLL):
        add_forces(last[2 * part], last[2 * part + 1], part)

    def gather_owners(index, carry):
        for source, start, target in (
            (row_sum, 0, own_force),
            (row_sum, half_tiles, other_force),
            *((col_sum, part * half_tiles, col_force.at[part]) for part in range(4)),
        ):
            for axis in range(3):
                target[index, axis] = source[
                    pl.ds(start + index * tiles_dev, tiles_dev), axis, :
                ]
        return carry

    lax.fori_loop(0, own_force.shape[0], gather_owners, 0)


def shards(positions, vel_half, charges, types, six_table, twelve_table, tile_pairs, pair_counts):
    atoms_dev = positions.shape[1]
    tiles_dev = TILES_DEV
    n_row = X_SIZE * ZH_SIZE * Y_SIZE
    n_col = N_COL
    n_xy = X_SIZE * Y_SIZE
    n_zl = n_col // CORES
    n_z = ZH_SIZE * n_zl
    my_zh = (lax.axis_index("row") // Y_SIZE) % ZH_SIZE
    my_zl = lax.axis_index("col") // CORES
    xy_groups = [
        [(x * ZH_SIZE + zh) * Y_SIZE + y for x in range(X_SIZE) for y in range(Y_SIZE)]
        for zh in range(ZH_SIZE)
    ]
    z_groups = [
        [
            ((x * ZH_SIZE + zh) * Y_SIZE + y) * n_col + zl * CORES + core
            for zh in range(ZH_SIZE)
            for zl in range(n_zl)
        ]
        for x in range(X_SIZE)
        for y in range(Y_SIZE)
        for core in range(CORES)
    ]
    core_swap = [(at, at ^ 1) for at in range(n_col)]

    smem = pl.BlockSpec(memory_space=pltpu.SMEM)
    vmem = pl.BlockSpec(memory_space=pltpu.VMEM)
    moved_pos, block, blocks = pl.pallas_call(
        pack_kernel,
        out_shape=(
            jax.ShapeDtypeStruct((3, atoms_dev), jnp.float32),
            jax.ShapeDtypeStruct((CHANNELS, tiles_dev, LANES), jnp.float32),
            jax.ShapeDtypeStruct((n_z, CHANNELS, tiles_dev, LANES), jnp.float32),
        ),
        in_specs=[vmem] * 4,
        out_specs=(vmem, vmem, vmem),
        name="pack_atoms",
    )(
        positions,
        vel_half,
        charges.reshape(tiles_dev, TILE_ATOMS),
        types.reshape(tiles_dev, TILE_ATOMS),
    )
    pad = ((0, TYPE_ROWS - BEAD_TYPES), (0, TYPE_ROWS - BEAD_TYPES))
    six = jnp.pad(six_table.T * (6.0 / CUT_SQ**2), pad)
    twelve = jnp.pad(twelve_table.T * (12.0 / CUT_SQ**2), pad)
    parts = []
    for table in (six, twelve):
        upper = lax.reduce_precision(table, 8, 7)
        parts += [upper, table - upper]
    tables = jnp.concatenate(parts, axis=0).astype(jnp.bfloat16)

    z_blocks = lax.all_to_all(blocks, ("row", "col"), 0, 0, axis_index_groups=z_groups)
    z_blocks, tables = lax.optimization_barrier((z_blocks, tables))
    other_blocks = lax.ppermute(z_blocks, "col", core_swap)
    far_block = lax.dynamic_index_in_dim(z_blocks, (1 - my_zh) * n_zl + my_zl, 0, keepdims=False)
    both = jnp.stack([block, far_block], axis=0)
    col_blocks = lax.all_to_all(
        jnp.broadcast_to(both[None], (n_xy, ZH_SIZE, CHANNELS, tiles_dev, LANES)),
        "row",
        0,
        0,
        axis_index_groups=xy_groups,
    )
    row_tiles = n_col * tiles_dev
    col_tiles = n_row * tiles_dev
    row_block, left_factors = pl.pallas_call(
        row_kernel,
        out_shape=(
            jax.ShapeDtypeStruct((row_tiles, 8, LANES), jnp.float32),
            jax.ShapeDtypeStruct((row_tiles, TILE_ATOMS, LANES), jnp.bfloat16),
        ),
        in_specs=[vmem, vmem, vmem],
        out_specs=(vmem, vmem),
        compiler_params=pltpu.CompilerParams(vmem_limit_bytes=16 * 2**20),
        cost_estimate=pl.CostEstimate(
            flops=2 * row_tiles * 96 * 128 * 128, bytes_accessed=4 * 2**20, transcendentals=0
        ),
        name="row_factors",
    )(z_blocks, other_blocks, tables)
    own_force, other_force, col_force = pl.pallas_call(
        pair_kernel,
        out_shape=(
            jax.ShapeDtypeStruct((n_zl, 3, tiles_dev, LANES), jnp.float32),
            jax.ShapeDtypeStruct((n_zl, 3, tiles_dev, LANES), jnp.float32),
            jax.ShapeDtypeStruct((n_row // n_zl, n_zl, 3, tiles_dev, LANES), jnp.float32),
        ),
        in_specs=[smem, smem, vmem, vmem, vmem],
        out_specs=(vmem, vmem, vmem),
        scratch_shapes=[
            pltpu.VMEM((col_tiles, 8, LANES), jnp.float32),
            pltpu.VMEM((row_tiles, 8, LANES), jnp.float32),
            pltpu.VMEM((col_tiles, 8, LANES), jnp.float32),
            pltpu.VMEM((UNROLL, 2, TILE_ATOMS, LANES), jnp.bfloat16),
        ],
        compiler_params=pltpu.CompilerParams(vmem_limit_bytes=24 * 2**20),
        name="pair_forces",
    )(tile_pairs, pair_counts, row_block, left_factors, col_blocks.reshape(n_row, CHANNELS, tiles_dev, LANES))
    core_force = lax.ppermute(other_force, "col", core_swap)
    col_parts = lax.all_to_all(
        col_force.reshape(n_xy, ZH_SIZE, 3, tiles_dev, LANES),
        "row",
        0,
        0,
        axis_index_groups=xy_groups,
    )
    col_sum = jnp.sum(col_parts, axis=0)
    row_sum = own_force + core_force
    to_zh = lax.broadcasted_iota(jnp.int32, (ZH_SIZE, n_zl, 3, tiles_dev, LANES), 0)
    to_zl = lax.broadcasted_iota(jnp.int32, (ZH_SIZE, n_zl, 3, tiles_dev, LANES), 1)
    far_sum = jnp.where(to_zl == my_zl, col_sum[1][None, None], 0.0)
    z_parts = lax.all_to_all(
        jnp.where(to_zh == my_zh, row_sum[None], far_sum).reshape(n_z, 3, tiles_dev, LANES),
        ("row", "col"),
        0,
        0,
        axis_index_groups=z_groups,
    )
    force = jnp.sum(z_parts, axis=0) + col_sum[0]
    force_new = force.reshape(3, atoms_dev)
    velocity_new = vel_half + HALF_KICK * force_new
    return (moved_pos, force_new, velocity_new)


def solution(mesh):
    placed = (
        P(None, ("row", "col")),
        P(None, ("row", "col")),
        P(("row", "col")),
        P(("row", "col")),
        P(),
        P(),
        P("row", "col", None, None),
        P("row", "col"),
    )
    return jax.shard_map(
        shards,
        mesh=mesh,
        in_specs=placed,
        out_specs=(P(None, ("row", "col")), P(None, ("row", "col")), P(None, ("row", "col"))),
        check_vma=False,
    )
```

time: 101 us -> 92 us (0.911)
  the two profiles are of different devices: /device:TPU:32 before, /device:TPU:8 now
where the time goes in v3:
time: 92 us; the launch traced here: 91.3 us
  starting transfers between devices  35.4 us (38%)
  waiting for transfers between devices  21.7 us (24%)
  blocking collectives  18.4 us (20%)
  Pallas kernels  10.3 us (11%)
  other arithmetic  3.04 us (3%)
  between operations  1.41 us (2%)
  local copies, waits for them, and re-layouts  1.15 us (1%)
    all_to_all x1, blocking collectives, shards(): lax.all_to_all(jnp.where(to_zh == my_zh, row_sum[None], far_sum).reshape(...  18.4 us
    all_to_all x1, starting transfers between devices, shards(): lax.all_to_all(blocks, ('row', 'col'), 0, 0, axis_index_groups=z_groups)  15.2 us
    all_to_all x1, waiting for transfers between devices, shards(): lax.all_to_all(blocks, ('row', 'col'), 0, 0, axis_index_groups=z_groups)  14.1 us
    all_to_all x1, starting transfers between devices, shards(): lax.all_to_all(col_force.reshape(n_xy, ZH_SIZE, 3, tiles_dev, LANES), 'ro...  8.99 us
    all_to_all x1, starting transfers between devices, shards(): lax.all_to_all(jnp.broadcast_to(both[None], (n_xy, ZH_SIZE, CHANNELS, til...  7.39 us
    pallas_call x1, Pallas kernels, shards(): pl.pallas_call(pair_kernel, out_shape=(jax.ShapeDtypeStruct((n_zl, 3, til...  7.26 us
    all_to_all x1, waiting for transfers between devices, shards(): lax.all_to_all(col_force.reshape(n_xy, ZH_SIZE, 3, tiles_dev, LANES), 'ro...  3.66 us
    all_to_all x1, waiting for transfers between devices, shards(): lax.all_to_all(jnp.broadcast_to(both[None], (n_xy, ZH_SIZE, CHANNELS, til...  2.42 us
  transfers between devices with their start and end apart: 5, of which 5 were waited for; matrix products, arithmetic and copies ran while one was open for 2% of the time, Pallas kernels for 2%

profile of v3, /device:TPU:8, one launch (start us, length us, event | category | flops | bytes accessed | tf_op | source)
XLA Modules:
  0.0 91.3 jit_solution(4159668667776761705)
XLA Ops:
  0.6 0.0 copy-start
  0.6 1.4 %pack_atoms.1 = (f32[3,512]{1,0:T(4,128)}, f32[5,4,128]{2,1,0:T(4,128)}, f32[16,5,4,128]{3,2,1,0:T(4,128)}) custom-call(f32[3,512]{1,0:T(4,128)} %positions_ref.1, f32[3,512]{1,0:T(4,128)} %vel_ref.1, f32[4,128]{1,0:T(4,128)} %bitcast.26, s32[4,128]{1,0:T(4,128)} %bitcast.27), custom_call_target="tpu_custom_call" | custom-call | tf_op jit(solution)/shard_map/pack_atoms/pallas_call | solution.py:284
  2.1 15.2 %all-to-all-start = ((f32[16,5,4,128]{3,2,1,0:T(4,128)}), f32[16,5,4,128]{3,2,1,0:T(4,128)S(1)}, u32[]{:S(2)}, u32[]{:S(2)}) async-start(f32[16,5,4,128]{3,2,1,0:T(4,128)} %get-tuple-element.14), calls=%async_computation | async-start | bytes 327680 | tf_op jit(solution)/shard_map/all_to_all | solution.py:309
  17.3 0.7 multiply_bitcast_fusion
  18.0 0.7 multiply_bitcast_fusion.1
  18.7 0.1 pad_maximum_fusion.1
  18.8 14.1 %all-to-all-done.own_ref = f32[16,5,4,128]{3,2,1,0:T(4,128)S(1)} async-done(((f32[16,5,4,128]{3,2,1,0:T(4,128)}), f32[16,5,4,128]{3,2,1,0:T(4,128)S(1)}, u32[]{:S(2)}, u32[]{:S(2)}) %all-to-all-start) | async-done | bytes 163872 | tf_op jit(solution)/shard_map/all_to_all | solution.py:309
  32.9 0.7 pad_maximum_fusion
  33.6 0.8 broadcast_in_dim.31
  34.4 7.4 %all-to-all-start.1 = ((f32[16,2,5,4,128]{4,3,2,1,0:T(4,128)}), f32[16,2,5,4,128]{4,3,2,1,0:T(4,128)S(1)}, u32[]{:S(2)}, u32[]{:S(2)}) async-start(f32[16,2,5,4,128]{4,3,2,1,0:T(4,128)} %broadcast_in_dim.31), calls=%async_computation.1 | async-start | bytes 655360 | tf_op jit(solution)/shard_map/all_to_all | solution.py:314
  41.8 1.9 %collective-permute-start = (f32[16,5,4,128]{3,2,1,0:T(4,128)S(1)}, f32[16,5,4,128]{3,2,1,0:T(4,128)S(1)}, u32[]{:S(2)}, u32[]{:S(2)}) collective-permute-start(f32[16,5,4,128]{3,2,1,0:T(4,128)S(1)} %all-to-all-done.own_ref), channel_id=1, source_target_pairs={{0,1},{1,0},{2,3},{3,2},{4,5},{5,4},{6,7},{7,6},{8,9},{9,8},{10,11... | collective-permute-start | bytes 491528 | tf_op jit(solution)/shard_map/ppermute | solution.py:311
  44.3 0.1 copy.16.table_ref
  44.4 0.6 collective-permute-done.other_ref
  45.1 1.6 %row_factors.1 = (f32[64,8,128]{2,1,0:T(8,128)S(1)}, bf16[64,128,128]{2,1,0:T(8,128)(2,1)S(1)}) custom-call(f32[16,5,4,128]{3,2,1,0:T(4,128)S(1)} %all-to-all-done.own_ref, f32[16,5,4,128]{3,2,1,0:T(4,128)S(1)} %collective-permute-done.other_ref, bf16[96,24]{1,0:T(8,128)(2,1)S(1)} %copy.16.table_ref), custom_call_target="tpu_custom_call" | custom-call | flops 201326592 | bytes 4194304 | tf_op jit(solution)/shard_map/row_factors/pallas_call | solution.py:323
  46.6 0.0 copy-start.1
  46.7 2.4 %all-to-all-done.1 = f32[16,2,5,4,128]{4,3,2,1,0:T(4,128)S(1)} async-done(((f32[16,2,5,4,128]{4,3,2,1,0:T(4,128)}), f32[16,2,5,4,128]{4,3,2,1,0:T(4,128)S(1)}, u32[]{:S(2)}, u32[]{:S(2)}) %all-to-all-start.1) | async-done | bytes 327712 | tf_op jit(solution)/shard_map/all_to_all | solution.py:314
  49.1 0.0 copy-done
  49.1 7.3 %pair_forces.1 = (f32[8,3,4,128]{3,2,1,0:T(4,128)S(1)}, f32[8,3,4,128]{3,2,1,0:T(4,128)S(1)}, f32[4,8,3,4,128]{4,3,2,1,0:T(4,128)}) custom-call(s32[1,1,2,128]{3,2,1,0:T(2,128)S(1)} %copy-done, s32[1,1]{1,0:T(1,128)S(6)} %copy.25.count_ref, f32[64,8,128]{2,1,0:T(8,128)S(1)} %get-tuple-element.17.row_block, ...), custom_call_target="tpu_custom_call" | custom-call | tf_op jit(solution)/shard_map/pair_forces/pallas_call | solution.py:337
  56.3 9.0 %all-to-all-start.2 = ((f32[16,2,3,4,128]{4,3,2,1,0:T(4,128)}), f32[16,2,3,4,128]{4,3,2,1,0:T(4,128)S(1)}, u32[]{:S(2)}, u32[]{:S(2)}) async-start(f32[16,2,3,4,128]{4,3,2,1,0:T(4,128)} %bitcast.7), calls=%async_computation.2 | async-start | bytes 393216 | tf_op jit(solution)/shard_map/all_to_all | solution.py:356
  65.3 1.9 %collective-permute-start.1 = (f32[8,3,4,128]{3,2,1,0:T(4,128)S(1)}, f32[8,3,4,128]{3,2,1,0:T(4,128)S(1)}, u32[]{:S(2)}, u32[]{:S(2)}) collective-permute-start(f32[8,3,4,128]{3,2,1,0:T(4,128)S(1)} %get-tuple-element.21), channel_id=1, source_target_pairs={{0,1},{1,0},{2,3},{3,2},{4,5},{5,4},{6,7},{7,6},{8,9},{9,8},{10,11... | collective-permute-start | bytes 147464 | tf_op jit(solution)/shard_map/ppermute | solution.py:355
  67.3 0.1 iota.26
  67.4 0.1 iota.21
  67.4 0.1 iota.22
  67.5 0.9 %collective-permute-done.1 = f32[8,3,4,128]{3,2,1,0:T(4,128)S(1)} collective-permute-done((f32[8,3,4,128]{3,2,1,0:T(4,128)S(1)}, f32[8,3,4,128]{3,2,1,0:T(4,128)S(1)}, u32[]{:S(2)}, u32[]{:S(2)}) %collective-permute-start.1) | collective-permute-done | bytes 49184 | tf_op jit(solution)/shard_map/ppermute | solution.py:355
  68.5 3.7 %all-to-all-done.2 = f32[16,2,3,4,128]{4,3,2,1,0:T(4,128)S(1)} async-done(((f32[16,2,3,4,128]{4,3,2,1,0:T(4,128)}), f32[16,2,3,4,128]{4,3,2,1,0:T(4,128)S(1)}, u32[]{:S(2)}, u32[]{:S(2)}) %all-to-all-start.2) | async-done | bytes 196640 | tf_op jit(solution)/shard_map/all_to_all | solution.py:356
  72.2 0.1 bitcast_select_fusion
  72.3 18.4 %all_to_all.20 = f32[16,3,4,128]{3,2,1,0:T(4,128)S(1)} all-to-all(f32[16,3,4,128]{3,2,1,0:T(4,128)S(1)} %bitcast_select_fusion), channel_id=1, replica_groups={{0,2,4,6,8,10,12,14,64,66,68,70,72,74,76,78},{1,3,5,7,9,11,13,15,65,67,..., dimensions={0} | all-to-all | bytes 196608 | tf_op jit(solution)/shard_map/all_to_all | solution.py:368
  90.7 0.0 copy-done.1
  90.7 0.6 multiply_add_fusion
  (9 shorter events, 0.1 us)
Async XLA Ops:
  0.6 48.4 %copy-start = (s32[1,1,2,128]{3,2,1,0:T(2,128)S(1)}, s32[1,1,2,128]{3,2,1,0:T(2,128)}, u32[]{:S(2)}) copy-start(s32[1,1,2,128]{3,2,1,0:T(2,128)} %pairs_ref.1) | copy-start | bytes 3076
  2.1 30.8 %all-to-all-start = ((f32[16,5,4,128]{3,2,1,0:T(4,128)}), f32[16,5,4,128]{3,2,1,0:T(4,128)S(1)}, u32[]{:S(2)}, u32[]{:S(2)}) async-start(f32[16,5,4,128]{3,2,1,0:T(4,128)} %get-tuple-element.14), calls=%async_computation | async-start | bytes 327680 | tf_op jit(solution)/shard_map/all_to_all | solution.py:309
  34.4 14.7 %all-to-all-start.1 = ((f32[16,2,5,4,128]{4,3,2,1,0:T(4,128)}), f32[16,2,5,4,128]{4,3,2,1,0:T(4,128)S(1)}, u32[]{:S(2)}, u32[]{:S(2)}) async-start(f32[16,2,5,4,128]{4,3,2,1,0:T(4,128)} %broadcast_in_dim.31), calls=%async_computation.1 | async-start | bytes 655360 | tf_op jit(solution)/shard_map/all_to_all | solution.py:314
  41.8 3.3 %collective-permute-start = (f32[16,5,4,128]{3,2,1,0:T(4,128)S(1)}, f32[16,5,4,128]{3,2,1,0:T(4,128)S(1)}, u32[]{:S(2)}, u32[]{:S(2)}) collective-permute-start(f32[16,5,4,128]{3,2,1,0:T(4,128)S(1)} %all-to-all-done.own_ref), channel_id=1, source_target_pairs={{0,1},{1,0},{2,3},{3,2},{4,5},{5,4},{6,7},{7,6},{8,9},{9,8},{10,11... | collective-permute-start | bytes 491528 | tf_op jit(solution)/shard_map/ppermute | solution.py:311
  46.6 44.1 %copy-start.1 = (f32[3,512]{1,0:T(4,128)S(1)}, f32[3,512]{1,0:T(4,128)}, u32[]{:S(2)}) copy-start(f32[3,512]{1,0:T(4,128)} %vel_ref.1) | copy-start | bytes 18436
  56.3 15.8 %all-to-all-start.2 = ((f32[16,2,3,4,128]{4,3,2,1,0:T(4,128)}), f32[16,2,3,4,128]{4,3,2,1,0:T(4,128)S(1)}, u32[]{:S(2)}, u32[]{:S(2)}) async-start(f32[16,2,3,4,128]{4,3,2,1,0:T(4,128)} %bitcast.7), calls=%async_computation.2 | async-start | bytes 393216 | tf_op jit(solution)/shard_map/all_to_all | solution.py:356
  65.3 3.1 %collective-permute-start.1 = (f32[8,3,4,128]{3,2,1,0:T(4,128)S(1)}, f32[8,3,4,128]{3,2,1,0:T(4,128)S(1)}, u32[]{:S(2)}, u32[]{:S(2)}) collective-permute-start(f32[8,3,4,128]{3,2,1,0:T(4,128)S(1)} %get-tuple-element.21), channel_id=1, source_target_pairs={{0,1},{1,0},{2,3},{3,2},{4,5},{5,4},{6,7},{7,6},{8,9},{9,8},{10,11... | collective-permute-start | bytes 147464 | tf_op jit(solution)/shard_map/ppermute | solution.py:355

commit v4 on v3

--- a/solution.py
+++ b/solution.py
@@ -36,7 +36,7 @@
     return upper, middle, rest - middle
 
 
-def pack_kernel(positions_ref, vel_ref, charge_ref, type_ref, moved_ref, block_ref, blocks_ref):
+def pack_kernel(positions_ref, vel_ref, charge_ref, type_ref, moved_ref, blocks_ref):
     moved = positions_ref[...] + TIME_STEP * vel_ref[...]
     moved_ref[...] = moved
     centred = moved - CENTRE
@@ -52,9 +52,31 @@
     ]
     channels += [charge_ref[...], type_ref[...].astype(jnp.float32)]
     for channel, values in enumerate(channels):
-        block_ref[channel] = values
         for copy in range(blocks_ref.shape[0]):
             blocks_ref[copy, channel] = values
+
+
+def join_kernel(z_ref, blocks_ref, own_ref):
+    n_zl = own_ref.shape[0]
+    my_zh = (lax.axis_index("row") // Y_SIZE) % ZH_SIZE
+    my_zl = lax.axis_index("col") // CORES
+    for half, zh in enumerate((my_zh, 1 - my_zh)):
+        block = z_ref[zh * n_zl + my_zl]
+        for copy in range(blocks_ref.shape[0]):
+            blocks_ref[copy, half] = block
+    for owner in range(n_zl):
+        own_ref[owner] = z_ref[my_zh * n_zl + owner]
+
+
+def table_kernel(six_ref, twelve_ref, pairs_ref, count_ref, table_ref, list_ref):
+    parts = []
+    for table, factor in ((six_ref, 6.0), (twelve_ref, 12.0)):
+        scaled = table[...] * (factor / CUT_SQ**2)
+        upper = scaled.astype(jnp.bfloat16).astype(jnp.float32)
+        parts += [upper, scaled - upper]
+    table_ref[...] = jnp.concatenate(parts, axis=0).astype(jnp.bfloat16)
+    list_ref[0:2] = pairs_ref[...]
+    list_ref[2:3] = jnp.broadcast_to(count_ref[...], (1, list_ref.shape[1]))
 
 
 def hot_types(block):
@@ -76,15 +98,12 @@
     sub8 = lax.broadcasted_iota(jnp.int32, (8, LANES), 0)
     scale = jnp.where(sub8 < 3, -2.0, jnp.where(sub8 == 4, COULOMB / CUT_SQ**2, 0.0)).astype(f32)
 
-    n_zl = own_ref.shape[0] // ZH_SIZE
-    start = ((lax.axis_index("row") // Y_SIZE) % ZH_SIZE) * n_zl
-
     def spread_owners(index, carry):
-        spread(own_ref, start + index, row_block, index * TILES_DEV)
-        spread(other_ref, start + index, row_block, half_tiles + index * TILES_DEV)
+        spread(own_ref, index, row_block, index * TILES_DEV)
+        spread(other_ref, index, row_block, half_tiles + index * TILES_DEV)
         return carry
 
-    lax.fori_loop(0, n_zl, spread_owners, 0)
+    lax.fori_loop(0, own_ref.shape[0], spread_owners, 0)
 
     def prepare(index, carry):
         wholes = []
@@ -108,7 +127,7 @@
 
 
 def pair_kernel(
-    pairs_ref, count_ref, row_block, lhs_ref, col_ref,
+    pairs_ref, row_block, lhs_ref, col_ref,
     own_force, other_force, col_force,
     col_block, row_sum, col_sum, scalar_ref
 ):
@@ -199,8 +218,8 @@
         col_sum[place] += right * sums_j[6:7] - sums_j
 
     def find(slot):
-        first = pairs_ref[0, 0, 0, slot]
-        second = pairs_ref[0, 0, 1, slot]
+        first = pairs_ref[0, slot]
+        second = pairs_ref[1, slot]
         owner = second >> 2
         tile = second & 3
         same = (owner == my_row) & (first == my_col * tiles_dev + tile)
@@ -233,7 +252,7 @@
         return tuple(place for first, second, _ in found for place in (first, second))
 
     last = lax.fori_loop(
-        0, count_ref[0, 0] // UNROLL, step, tuple(jnp.int32(0) for _ in range(2 * UNROLL))
+        0, pairs_ref[2, 0] // UNROLL, step, tuple(jnp.int32(0) for _ in range(2 * UNROLL))
     )
     for part in range(UNROLL):
         add_forces(last[2 * part], last[2 * part + 1], part)
@@ -261,8 +280,8 @@
     n_xy = X_SIZE * Y_SIZE
     n_zl = n_col // CORES
     n_z = ZH_SIZE * n_zl
-    my_zh = (lax.axis_index("row") // Y_SIZE) % ZH_SIZE
-    my_zl = lax.axis_index("col") // CORES
+    my_zh = (lax.axis_index("row") >> 2) & 1
+    my_zl = lax.axis_index("col") >> 1
     xy_groups = [
         [(x * ZH_SIZE + zh) * Y_SIZE + y for x in range(X_SIZE) for y in range(Y_SIZE)]
         for zh in range(ZH_SIZE)
@@ -281,15 +300,14 @@
 
     smem = pl.BlockSpec(memory_space=pltpu.SMEM)
     vmem = pl.BlockSpec(memory_space=pltpu.VMEM)
-    moved_pos, block, blocks = pl.pallas_call(
+    moved_pos, blocks = pl.pallas_call(
         pack_kernel,
         out_shape=(
             jax.ShapeDtypeStruct((3, atoms_dev), jnp.float32),
-            jax.ShapeDtypeStruct((CHANNELS, tiles_dev, LANES), jnp.float32),
             jax.ShapeDtypeStruct((n_z, CHANNELS, tiles_dev, LANES), jnp.float32),
         ),
         in_specs=[vmem] * 4,
-        out_specs=(vmem, vmem, vmem),
+        out_specs=(vmem, vmem),
         name="pack_atoms",
     )(
         positions,
@@ -298,26 +316,37 @@
         types.reshape(tiles_dev, TILE_ATOMS),
     )
     pad = ((0, TYPE_ROWS - BEAD_TYPES), (0, TYPE_ROWS - BEAD_TYPES))
-    six = jnp.pad(six_table.T * (6.0 / CUT_SQ**2), pad)
-    twelve = jnp.pad(twelve_table.T * (12.0 / CUT_SQ**2), pad)
-    parts = []
-    for table in (six, twelve):
-        upper = lax.reduce_precision(table, 8, 7)
-        parts += [upper, table - upper]
-    tables = jnp.concatenate(parts, axis=0).astype(jnp.bfloat16)
-
+    tables, pair_list = pl.pallas_call(
+        table_kernel,
+        out_shape=(
+            jax.ShapeDtypeStruct((4 * TYPE_ROWS, TYPE_ROWS), jnp.bfloat16),
+            jax.ShapeDtypeStruct((3, tile_pairs.shape[3]), jnp.int32),
+        ),
+        in_specs=[vmem] * 4,
+        out_specs=(vmem, vmem),
+        compiler_params=pltpu.CompilerParams(vmem_limit_bytes=4 * 2**20),
+        name="tables",
+    )(
+        jnp.pad(six_table.T, pad),
+        jnp.pad(twelve_table.T, pad),
+        tile_pairs[0, 0],
+        pair_counts,
+    )
     z_blocks = lax.all_to_all(blocks, ("row", "col"), 0, 0, axis_index_groups=z_groups)
-    z_blocks, tables = lax.optimization_barrier((z_blocks, tables))
-    other_blocks = lax.ppermute(z_blocks, "col", core_swap)
-    far_block = lax.dynamic_index_in_dim(z_blocks, (1 - my_zh) * n_zl + my_zl, 0, keepdims=False)
-    both = jnp.stack([block, far_block], axis=0)
-    col_blocks = lax.all_to_all(
-        jnp.broadcast_to(both[None], (n_xy, ZH_SIZE, CHANNELS, tiles_dev, LANES)),
-        "row",
-        0,
-        0,
-        axis_index_groups=xy_groups,
-    )
+    z_blocks, tables, pair_list = lax.optimization_barrier((z_blocks, tables, pair_list))
+    both, own_blocks = pl.pallas_call(
+        join_kernel,
+        out_shape=(
+            jax.ShapeDtypeStruct((n_xy, ZH_SIZE, CHANNELS, tiles_dev, LANES), jnp.float32),
+            jax.ShapeDtypeStruct((n_zl, CHANNELS, tiles_dev, LANES), jnp.float32),
+        ),
+        in_specs=[vmem],
+        out_specs=(vmem, vmem),
+        compiler_params=pltpu.CompilerParams(vmem_limit_bytes=4 * 2**20),
+        name="join_halves",
+    )(z_blocks)
+    col_blocks = lax.all_to_all(both, "row", 0, 0, axis_index_groups=xy_groups)
+    other_blocks = lax.ppermute(own_blocks, "col", core_swap)
     row_tiles = n_col * tiles_dev
     col_tiles = n_row * tiles_dev
     row_block, left_factors = pl.pallas_call(
@@ -333,7 +362,7 @@
             flops=2 * row_tiles * 96 * 128 * 128, bytes_accessed=4 * 2**20, transcendentals=0
         ),
         name="row_factors",
-    )(z_blocks, other_blocks, tables)
+    )(own_blocks, other_blocks, tables)
     own_force, other_force, col_force = pl.pallas_call(
         pair_kernel,
         out_shape=(
@@ -341,7 +370,7 @@
             jax.ShapeDtypeStruct((n_zl, 3, tiles_dev, LANES), jnp.float32),
             jax.ShapeDtypeStruct((n_row // n_zl, n_zl, 3, tiles_dev, LANES), jnp.float32),
         ),
-        in_specs=[smem, smem, vmem, vmem, vmem],
+        in_specs=[smem, vmem, vmem, vmem],
         out_specs=(vmem, vmem, vmem),
         scratch_shapes=[
             pltpu.VMEM((col_tiles, 8, LANES), jnp.float32),
@@ -351,7 +380,7 @@
         ],
         compiler_params=pltpu.CompilerParams(vmem_limit_bytes=24 * 2**20),
         name="pair_forces",
-    )(tile_pairs, pair_counts, row_block, left_factors, col_blocks.reshape(n_row, CHANNELS, tiles_dev, LANES))
+    )(pair_list, row_block, left_factors, col_blocks.reshape(n_row, CHANNELS, tiles_dev, LANES))
     core_force = lax.ppermute(other_force, "col", core_swap)
     col_parts = lax.all_to_all(
         col_force.reshape(n_xy, ZH_SIZE, 3, tiles_dev, LANES),

time: 92 us -> 91.2 us (level)
  the two profiles are of different devices: /device:TPU:8 before, /device:TPU:32 now
where the time goes in v4:
time: 91.2 us; the launch traced here: 90.4 us
  starting transfers between devices  34.5 us (38%)
  waiting for transfers between devices  23 us (25%)
  blocking collectives  17.1 us (19%)
  Pallas kernels  11.1 us (12%)
  local copies, waits for them, and re-layouts  2.54 us (3%)
  between operations  1.38 us (2%)
    all_to_all x1, blocking collectives, shards(): lax.all_to_all(jnp.where(to_zh == my_zh, row_sum[None], far_sum).reshape(...  17.1 us
    all_to_all x1, starting transfers between devices, shards(): lax.all_to_all(blocks, ('row', 'col'), 0, 0, axis_index_groups=z_groups)  15.2 us
    all_to_all x1, waiting for transfers between devices, shards(): lax.all_to_all(blocks, ('row', 'col'), 0, 0, axis_index_groups=z_groups)  11.8 us
    all_to_all x1, starting transfers between devices, shards(): lax.all_to_all(col_force.reshape(n_xy, ZH_SIZE, 3, tiles_dev, LANES), 'ro...  8.4 us
    pallas_call x1, Pallas kernels, shards(): pl.pallas_call(pair_kernel, out_shape=(jax.ShapeDtypeStruct((n_zl, 3, til...  7.28 us
    all_to_all x1, starting transfers between devices, shards(): col_blocks = lax.all_to_all(both, 'row', 0, 0, axis_index_groups=xy_groups)  7.03 us
    all_to_all x1, waiting for transfers between devices, shards(): lax.all_to_all(col_force.reshape(n_xy, ZH_SIZE, 3, tiles_dev, LANES), 'ro...  4.92 us
    all_to_all x1, waiting for transfers between devices, shards(): col_blocks = lax.all_to_all(both, 'row', 0, 0, axis_index_groups=xy_groups)  4.04 us
  transfers between devices with their start and end apart: 5, of which 5 were waited for; matrix products, arithmetic and copies ran while one was open for 2% of the time, Pallas kernels for 2%

profile of v4, /device:TPU:32, one launch (start us, length us, event | category | flops | bytes accessed | tf_op | source)
XLA Modules:
  0.0 90.4 jit_solution(54106834884696354)
XLA Ops:
  0.6 1.4 %pack_atoms.1 = (f32[3,512]{1,0:T(4,128)}, f32[16,5,4,128]{3,2,1,0:T(4,128)}) custom-call(f32[3,512]{1,0:T(4,128)} %positions_ref.1, f32[3,512]{1,0:T(4,128)} %vel_ref.1, f32[4,128]{1,0:T(4,128)} %bitcast.26, s32[4,128]{1,0:T(4,128)} %bitcast.27), custom_call_target="tpu_custom_call" | custom-call | tf_op jit(solution)/shard_map/pack_atoms/pallas_call | solution.py:303
  2.0 15.2 %all-to-all-start = ((f32[16,5,4,128]{3,2,1,0:T(4,128)}), f32[16,5,4,128]{3,2,1,0:T(4,128)S(1)}, u32[]{:S(2)}, u32[]{:S(2)}) async-start(f32[16,5,4,128]{3,2,1,0:T(4,128)} %get-tuple-element.18), calls=%async_computation | async-start | bytes 327680 | tf_op jit(solution)/shard_map/all_to_all | solution.py:335
  17.9 0.8 copy.16
  18.7 0.8 copy.17
  19.5 0.0 copy-start
  19.5 0.7 copy-done
  20.2 0.1 tables.1
  20.3 11.8 %all-to-all-done.z_ref = f32[16,5,4,128]{3,2,1,0:T(4,128)S(1)} async-done(((f32[16,5,4,128]{3,2,1,0:T(4,128)}), f32[16,5,4,128]{3,2,1,0:T(4,128)S(1)}, u32[]{:S(2)}, u32[]{:S(2)}) %all-to-all-start) | async-done | bytes 163872 | tf_op jit(solution)/shard_map/all_to_all | solution.py:335
  32.1 0.8 join_halves.1
  32.9 7.0 %all-to-all-start.1 = ((f32[16,2,5,4,128]{4,3,2,1,0:T(4,128)}), f32[16,2,5,4,128]{4,3,2,1,0:T(4,128)S(1)}, u32[]{:S(2)}, u32[]{:S(2)}) async-start(f32[16,2,5,4,128]{4,3,2,1,0:T(4,128)} %get-tuple-element.27), calls=%async_computation.1 | async-start | bytes 655360 | tf_op jit(solution)/shard_map/all_to_all | solution.py:348
  39.9 1.9 %collective-permute-start = (f32[8,5,4,128]{3,2,1,0:T(4,128)S(1)}, f32[8,5,4,128]{3,2,1,0:T(4,128)S(1)}, u32[]{:S(2)}, u32[]{:S(2)}) collective-permute-start(f32[8,5,4,128]{3,2,1,0:T(4,128)S(1)} %get-tuple-element.23.own_ref), channel_id=1, source_target_pairs={{0,1},{1,0},{2,3},{3,2},{4,5},{5,4},{6,7},{7,6},{8,9},{9,8},{10,11... | collective-permute-start | bytes 245768 | tf_op jit(solution)/shard_map/ppermute | solution.py:349
  41.9 1.2 %collective-permute-done.other_ref = f32[8,5,4,128]{3,2,1,0:T(4,128)S(1)} collective-permute-done((f32[8,5,4,128]{3,2,1,0:T(4,128)S(1)}, f32[8,5,4,128]{3,2,1,0:T(4,128)S(1)}, u32[]{:S(2)}, u32[]{:S(2)}) %collective-permute-start) | collective-permute-done | bytes 81952 | tf_op jit(solution)/shard_map/ppermute | solution.py:349
  43.1 1.6 %row_factors.1 = (f32[64,8,128]{2,1,0:T(8,128)S(1)}, bf16[64,128,128]{2,1,0:T(8,128)(2,1)S(1)}) custom-call(f32[8,5,4,128]{3,2,1,0:T(4,128)S(1)} %get-tuple-element.23.own_ref, f32[8,5,4,128]{3,2,1,0:T(4,128)S(1)} %collective-permute-done.other_ref, bf16[96,24]{1,0:T(8,128)(2,1)S(1)} %get-tuple-element.24.table_ref), custom_call_target="tpu_custom_call" | custom-call | flops 201326592 | bytes 4194304 | tf_op jit(solution)/shard_map/row_factors/pallas_call | solution.py:352
  44.7 0.0 copy-start.1
  44.7 4.0 %all-to-all-done.1 = f32[16,2,5,4,128]{4,3,2,1,0:T(4,128)S(1)} async-done(((f32[16,2,5,4,128]{4,3,2,1,0:T(4,128)}), f32[16,2,5,4,128]{4,3,2,1,0:T(4,128)S(1)}, u32[]{:S(2)}, u32[]{:S(2)}) %all-to-all-start.1) | async-done | bytes 327712 | tf_op jit(solution)/shard_map/all_to_all | solution.py:348
  48.8 7.3 %pair_forces.1 = (f32[8,3,4,128]{3,2,1,0:T(4,128)S(1)}, f32[8,3,4,128]{3,2,1,0:T(4,128)S(1)}, f32[4,8,3,4,128]{4,3,2,1,0:T(4,128)}) custom-call(s32[3,128]{1,0:T(4,128)S(1)} %get-tuple-element.21.pairs_ref, f32[64,8,128]{2,1,0:T(8,128)S(1)} %get-tuple-element.25.row_block, bf16[64,128,128]{2,1,0:T(8,128)(2,1)S(1)} %get-tuple-element.26.lhs_ref, ...), custom_call_target="tpu_custom_call" | custom-call | tf_op jit(solution)/shard_map/pair_forces/pallas_call | solution.py:366
  56.0 8.4 %all-to-all-start.2 = ((f32[16,2,3,4,128]{4,3,2,1,0:T(4,128)}), f32[16,2,3,4,128]{4,3,2,1,0:T(4,128)S(1)}, u32[]{:S(2)}, u32[]{:S(2)}) async-start(f32[16,2,3,4,128]{4,3,2,1,0:T(4,128)} %bitcast.7), calls=%async_computation.2 | async-start | bytes 393216 | tf_op jit(solution)/shard_map/all_to_all | solution.py:385
  64.5 1.9 %collective-permute-start.1 = (f32[8,3,4,128]{3,2,1,0:T(4,128)S(1)}, f32[8,3,4,128]{3,2,1,0:T(4,128)S(1)}, u32[]{:S(2)}, u32[]{:S(2)}) collective-permute-start(f32[8,3,4,128]{3,2,1,0:T(4,128)S(1)} %get-tuple-element.29), channel_id=1, source_target_pairs={{0,1},{1,0},{2,3},{3,2},{4,5},{5,4},{6,7},{7,6},{8,9},{9,8},{10,11... | collective-permute-start | bytes 147464 | tf_op jit(solution)/shard_map/ppermute | solution.py:384
  66.4 0.1 iota.21
  66.5 0.1 iota.22
  66.6 0.1 iota.26
  66.7 0.9 %collective-permute-done.1 = f32[8,3,4,128]{3,2,1,0:T(4,128)S(1)} collective-permute-done((f32[8,3,4,128]{3,2,1,0:T(4,128)S(1)}, f32[8,3,4,128]{3,2,1,0:T(4,128)S(1)}, u32[]{:S(2)}, u32[]{:S(2)}) %collective-permute-start.1) | collective-permute-done | bytes 49184 | tf_op jit(solution)/shard_map/ppermute | solution.py:384
  67.6 4.9 %all-to-all-done.2 = f32[16,2,3,4,128]{4,3,2,1,0:T(4,128)S(1)} async-done(((f32[16,2,3,4,128]{4,3,2,1,0:T(4,128)}), f32[16,2,3,4,128]{4,3,2,1,0:T(4,128)S(1)}, u32[]{:S(2)}, u32[]{:S(2)}) %all-to-all-start.2) | async-done | bytes 196640 | tf_op jit(solution)/shard_map/all_to_all | solution.py:385
  72.6 0.1 bitcast_select_fusion
  72.7 17.1 %all_to_all.20 = f32[16,3,4,128]{3,2,1,0:T(4,128)S(1)} all-to-all(f32[16,3,4,128]{3,2,1,0:T(4,128)S(1)} %bitcast_select_fusion), channel_id=1, replica_groups={{0,2,4,6,8,10,12,14,64,66,68,70,72,74,76,78},{1,3,5,7,9,11,13,15,65,67,..., dimensions={0} | all-to-all | bytes 196608 | tf_op jit(solution)/shard_map/all_to_all | solution.py:397
  89.8 0.0 copy-done.1
  89.8 0.6 multiply_add_fusion
  (9 shorter events, 0.1 us)
Async XLA Ops:
  2.0 30.1 %all-to-all-start = ((f32[16,5,4,128]{3,2,1,0:T(4,128)}), f32[16,5,4,128]{3,2,1,0:T(4,128)S(1)}, u32[]{:S(2)}, u32[]{:S(2)}) async-start(f32[16,5,4,128]{3,2,1,0:T(4,128)} %get-tuple-element.18), calls=%async_computation | async-start | bytes 327680 | tf_op jit(solution)/shard_map/all_to_all | solution.py:335
  19.5 0.7 copy-start
  32.9 15.9 %all-to-all-start.1 = ((f32[16,2,5,4,128]{4,3,2,1,0:T(4,128)}), f32[16,2,5,4,128]{4,3,2,1,0:T(4,128)S(1)}, u32[]{:S(2)}, u32[]{:S(2)}) async-start(f32[16,2,5,4,128]{4,3,2,1,0:T(4,128)} %get-tuple-element.27), calls=%async_computation.1 | async-start | bytes 655360 | tf_op jit(solution)/shard_map/all_to_all | solution.py:348
  39.9 3.2 %collective-permute-start = (f32[8,5,4,128]{3,2,1,0:T(4,128)S(1)}, f32[8,5,4,128]{3,2,1,0:T(4,128)S(1)}, u32[]{:S(2)}, u32[]{:S(2)}) collective-permute-start(f32[8,5,4,128]{3,2,1,0:T(4,128)S(1)} %get-tuple-element.23.own_ref), channel_id=1, source_target_pairs={{0,1},{1,0},{2,3},{3,2},{4,5},{5,4},{6,7},{7,6},{8,9},{9,8},{10,11... | collective-permute-start | bytes 245768 | tf_op jit(solution)/shard_map/ppermute | solution.py:349
  44.7 45.1 %copy-start.1 = (f32[3,512]{1,0:T(4,128)S(1)}, f32[3,512]{1,0:T(4,128)}, u32[]{:S(2)}) copy-start(f32[3,512]{1,0:T(4,128)} %vel_ref.1) | copy-start | bytes 18436
  56.0 16.5 %all-to-all-start.2 = ((f32[16,2,3,4,128]{4,3,2,1,0:T(4,128)}), f32[16,2,3,4,128]{4,3,2,1,0:T(4,128)S(1)}, u32[]{:S(2)}, u32[]{:S(2)}) async-start(f32[16,2,3,4,128]{4,3,2,1,0:T(4,128)} %bitcast.7), calls=%async_computation.2 | async-start | bytes 393216 | tf_op jit(solution)/shard_map/all_to_all | solution.py:385
  64.5 3.1 %collective-permute-start.1 = (f32[8,3,4,128]{3,2,1,0:T(4,128)S(1)}, f32[8,3,4,128]{3,2,1,0:T(4,128)S(1)}, u32[]{:S(2)}, u32[]{:S(2)}) collective-permute-start(f32[8,3,4,128]{3,2,1,0:T(4,128)S(1)} %get-tuple-element.29), channel_id=1, source_target_pairs={{0,1},{1,0},{2,3},{3,2},{4,5},{5,4},{6,7},{7,6},{8,9},{9,8},{10,11... | collective-permute-start | bytes 147464 | tf_op jit(solution)/shard_map/ppermute | solution.py:384

commit v5 on v4

--- a/solution.py
+++ b/solution.py
@@ -27,7 +27,7 @@
 CHANNELS = 5
 TYPE_ROWS = 24
 UNROLL = 16
-PREPARED = 16
+PREPARED = 32
 
 def split_three(values):
     upper = values.astype(jnp.bfloat16).astype(jnp.float32)
@@ -103,7 +103,7 @@
         spread(other_ref, index, row_block, half_tiles + index * TILES_DEV)
         return carry
 
-    lax.fori_loop(0, own_ref.shape[0], spread_owners, 0)
+    lax.fori_loop(0, own_ref.shape[0], spread_owners, 0, unroll=True)
 
     def prepare(index, carry):
         wholes = []
@@ -269,7 +269,7 @@
                 ]
         return carry
 
-    lax.fori_loop(0, own_force.shape[0], gather_owners, 0)
+    lax.fori_loop(0, own_force.shape[0], gather_owners, 0, unroll=True)
 
 
 def shards(positions, vel_half, charges, types, six_table, twelve_table, tile_pairs, pair_counts):

time: 91.2 us -> 91.1 us (level)
  the two profiles are of different devices: /device:TPU:32 before, /device:TPU:2 now
where the time goes in v5:
time: 91.1 us; the launch traced here: 90.4 us
  starting transfers between devices  31.1 us (34%)
  waiting for transfers between devices  20.9 us (23%)
  blocking collectives  18.2 us (20%)
  Pallas kernels  15.4 us (17%)
  local copies, waits for them, and re-layouts  2.54 us (3%)
  between operations  1.36 us (1%)
    all_to_all x1, blocking collectives, shards(): lax.all_to_all(jnp.where(to_zh == my_zh, row_sum[None], far_sum).reshape(...  18.2 us
    all_to_all x1, starting transfers between devices, shards(): lax.all_to_all(blocks, ('row', 'col'), 0, 0, axis_index_groups=z_groups)  15.2 us
    all_to_all x1, waiting for transfers between devices, shards(): lax.all_to_all(blocks, ('row', 'col'), 0, 0, axis_index_groups=z_groups)  12.6 us
    pallas_call x1, Pallas kernels, shards(): pl.pallas_call(pair_kernel, out_shape=(jax.ShapeDtypeStruct((n_zl, 3, til...  12 us
    all_to_all x1, starting transfers between devices, shards(): col_blocks = lax.all_to_all(both, 'row', 0, 0, axis_index_groups=xy_groups)  7.48 us
    all_to_all x1, starting transfers between devices, shards(): lax.all_to_all(col_force.reshape(n_xy, ZH_SIZE, 3, tiles_dev, LANES), 'ro...  4.62 us
    all_to_all x1, waiting for transfers between devices, shards(): lax.all_to_all(col_force.reshape(n_xy, ZH_SIZE, 3, tiles_dev, LANES), 'ro...  3.43 us
    all_to_all x1, waiting for transfers between devices, shards(): col_blocks = lax.all_to_all(both, 'row', 0, 0, axis_index_groups=xy_groups)  2.71 us
  transfers between devices with their start and end apart: 5, of which 5 were waited for; matrix products, arithmetic and copies ran while one was open for 2% of the time, Pallas kernels for 1%

profile of v5, /device:TPU:2, one launch (start us, length us, event | category | flops | bytes accessed | tf_op | source)
XLA Modules:
  0.0 90.4 jit_solution(2967230777628607596)
XLA Ops:
  0.6 1.4 %pack_atoms.1 = (f32[3,512]{1,0:T(4,128)}, f32[16,5,4,128]{3,2,1,0:T(4,128)}) custom-call(f32[3,512]{1,0:T(4,128)} %positions_ref.1, f32[3,512]{1,0:T(4,128)} %vel_ref.1, f32[4,128]{1,0:T(4,128)} %bitcast.26, s32[4,128]{1,0:T(4,128)} %bitcast.27), custom_call_target="tpu_custom_call" | custom-call | tf_op jit(solution)/shard_map/pack_atoms/pallas_call | solution.py:303
  2.0 15.2 %all-to-all-start = ((f32[16,5,4,128]{3,2,1,0:T(4,128)}), f32[16,5,4,128]{3,2,1,0:T(4,128)S(1)}, u32[]{:S(2)}, u32[]{:S(2)}) async-start(f32[16,5,4,128]{3,2,1,0:T(4,128)} %get-tuple-element.18), calls=%async_computation | async-start | bytes 327680 | tf_op jit(solution)/shard_map/all_to_all | solution.py:335
  17.9 0.8 copy.16
  18.7 0.8 copy.17
  19.5 0.0 copy-start
  19.5 0.7 copy-done
  20.2 0.1 tables.1
  20.3 12.6 %all-to-all-done.z_ref = f32[16,5,4,128]{3,2,1,0:T(4,128)S(1)} async-done(((f32[16,5,4,128]{3,2,1,0:T(4,128)}), f32[16,5,4,128]{3,2,1,0:T(4,128)S(1)}, u32[]{:S(2)}, u32[]{:S(2)}) %all-to-all-start) | async-done | bytes 163872 | tf_op jit(solution)/shard_map/all_to_all | solution.py:335
  32.9 0.8 join_halves.1
  33.7 7.5 %all-to-all-start.1 = ((f32[16,2,5,4,128]{4,3,2,1,0:T(4,128)}), f32[16,2,5,4,128]{4,3,2,1,0:T(4,128)S(1)}, u32[]{:S(2)}, u32[]{:S(2)}) async-start(f32[16,2,5,4,128]{4,3,2,1,0:T(4,128)} %get-tuple-element.27), calls=%async_computation.1 | async-start | bytes 655360 | tf_op jit(solution)/shard_map/all_to_all | solution.py:348
  41.1 1.9 %collective-permute-start = (f32[8,5,4,128]{3,2,1,0:T(4,128)S(1)}, f32[8,5,4,128]{3,2,1,0:T(4,128)S(1)}, u32[]{:S(2)}, u32[]{:S(2)}) collective-permute-start(f32[8,5,4,128]{3,2,1,0:T(4,128)S(1)} %get-tuple-element.23.own_ref), channel_id=1, source_target_pairs={{0,1},{1,0},{2,3},{3,2},{4,5},{5,4},{6,7},{7,6},{8,9},{9,8},{10,11... | collective-permute-start | bytes 245768 | tf_op jit(solution)/shard_map/ppermute | solution.py:349
  43.1 1.2 %collective-permute-done.other_ref = f32[8,5,4,128]{3,2,1,0:T(4,128)S(1)} collective-permute-done((f32[8,5,4,128]{3,2,1,0:T(4,128)S(1)}, f32[8,5,4,128]{3,2,1,0:T(4,128)S(1)}, u32[]{:S(2)}, u32[]{:S(2)}) %collective-permute-start) | collective-permute-done | bytes 81952 | tf_op jit(solution)/shard_map/ppermute | solution.py:349
  44.3 1.1 %row_factors.1 = (f32[64,8,128]{2,1,0:T(8,128)S(1)}, bf16[64,128,128]{2,1,0:T(8,128)(2,1)S(1)}) custom-call(f32[8,5,4,128]{3,2,1,0:T(4,128)S(1)} %get-tuple-element.23.own_ref, f32[8,5,4,128]{3,2,1,0:T(4,128)S(1)} %collective-permute-done.other_ref, bf16[96,24]{1,0:T(8,128)(2,1)S(1)} %get-tuple-element.24.table_ref), custom_call_target="tpu_custom_call" | custom-call | flops 201326592 | bytes 4194304 | tf_op jit(solution)/shard_map/row_factors/pallas_call | solution.py:352
  45.4 0.0 copy-start.1
  45.5 2.7 %all-to-all-done.1 = f32[16,2,5,4,128]{4,3,2,1,0:T(4,128)S(1)} async-done(((f32[16,2,5,4,128]{4,3,2,1,0:T(4,128)}), f32[16,2,5,4,128]{4,3,2,1,0:T(4,128)S(1)}, u32[]{:S(2)}, u32[]{:S(2)}) %all-to-all-start.1) | async-done | bytes 327712 | tf_op jit(solution)/shard_map/all_to_all | solution.py:348
  48.2 12.0 %pair_forces.1 = (f32[8,3,4,128]{3,2,1,0:T(4,128)S(1)}, f32[8,3,4,128]{3,2,1,0:T(4,128)S(1)}, f32[4,8,3,4,128]{4,3,2,1,0:T(4,128)}) custom-call(s32[3,128]{1,0:T(4,128)S(1)} %get-tuple-element.21.pairs_ref, f32[64,8,128]{2,1,0:T(8,128)S(1)} %get-tuple-element.25.row_block, bf16[64,128,128]{2,1,0:T(8,128)(2,1)S(1)} %get-tuple-element.26.lhs_ref, ...), custom_call_target="tpu_custom_call" | custom-call | tf_op jit(solution)/shard_map/pair_forces/pallas_call | solution.py:366
  60.2 4.6 %all-to-all-start.2 = ((f32[16,2,3,4,128]{4,3,2,1,0:T(4,128)}), f32[16,2,3,4,128]{4,3,2,1,0:T(4,128)S(1)}, u32[]{:S(2)}, u32[]{:S(2)}) async-start(f32[16,2,3,4,128]{4,3,2,1,0:T(4,128)} %bitcast.7), calls=%async_computation.2 | async-start | bytes 393216 | tf_op jit(solution)/shard_map/all_to_all | solution.py:385
  64.8 1.9 %collective-permute-start.1 = (f32[8,3,4,128]{3,2,1,0:T(4,128)S(1)}, f32[8,3,4,128]{3,2,1,0:T(4,128)S(1)}, u32[]{:S(2)}, u32[]{:S(2)}) collective-permute-start(f32[8,3,4,128]{3,2,1,0:T(4,128)S(1)} %get-tuple-element.29), channel_id=1, source_target_pairs={{0,1},{1,0},{2,3},{3,2},{4,5},{5,4},{6,7},{7,6},{8,9},{9,8},{10,11... | collective-permute-start | bytes 147464 | tf_op jit(solution)/shard_map/ppermute | solution.py:384
  66.7 0.1 iota.21
  66.8 0.1 iota.22
  66.9 0.1 iota.26
  67.0 0.9 %collective-permute-done.1 = f32[8,3,4,128]{3,2,1,0:T(4,128)S(1)} collective-permute-done((f32[8,3,4,128]{3,2,1,0:T(4,128)S(1)}, f32[8,3,4,128]{3,2,1,0:T(4,128)S(1)}, u32[]{:S(2)}, u32[]{:S(2)}) %collective-permute-start.1) | collective-permute-done | bytes 49184 | tf_op jit(solution)/shard_map/ppermute | solution.py:384
  67.9 3.4 %all-to-all-done.2 = f32[16,2,3,4,128]{4,3,2,1,0:T(4,128)S(1)} async-done(((f32[16,2,3,4,128]{4,3,2,1,0:T(4,128)}), f32[16,2,3,4,128]{4,3,2,1,0:T(4,128)S(1)}, u32[]{:S(2)}, u32[]{:S(2)}) %all-to-all-start.2) | async-done | bytes 196640 | tf_op jit(solution)/shard_map/all_to_all | solution.py:385
  71.4 0.1 bitcast_select_fusion
  71.5 18.2 %all_to_all.20 = f32[16,3,4,128]{3,2,1,0:T(4,128)S(1)} all-to-all(f32[16,3,4,128]{3,2,1,0:T(4,128)S(1)} %bitcast_select_fusion), channel_id=1, replica_groups={{0,2,4,6,8,10,12,14,64,66,68,70,72,74,76,78},{1,3,5,7,9,11,13,15,65,67,..., dimensions={0} | all-to-all | bytes 196608 | tf_op jit(solution)/shard_map/all_to_all | solution.py:397
  89.8 0.0 copy-done.1
  89.8 0.6 multiply_add_fusion
  (9 shorter events, 0.1 us)
Async XLA Ops:
  2.0 30.8 %all-to-all-start = ((f32[16,5,4,128]{3,2,1,0:T(4,128)}), f32[16,5,4,128]{3,2,1,0:T(4,128)S(1)}, u32[]{:S(2)}, u32[]{:S(2)}) async-start(f32[16,5,4,128]{3,2,1,0:T(4,128)} %get-tuple-element.18), calls=%async_computation | async-start | bytes 327680 | tf_op jit(solution)/shard_map/all_to_all | solution.py:335
  19.5 0.7 copy-start
  33.7 14.5 %all-to-all-start.1 = ((f32[16,2,5,4,128]{4,3,2,1,0:T(4,128)}), f32[16,2,5,4,128]{4,3,2,1,0:T(4,128)S(1)}, u32[]{:S(2)}, u32[]{:S(2)}) async-start(f32[16,2,5,4,128]{4,3,2,1,0:T(4,128)} %get-tuple-element.27), calls=%async_computation.1 | async-start | bytes 655360 | tf_op jit(solution)/shard_map/all_to_all | solution.py:348
  41.1 3.2 %collective-permute-start = (f32[8,5,4,128]{3,2,1,0:T(4,128)S(1)}, f32[8,5,4,128]{3,2,1,0:T(4,128)S(1)}, u32[]{:S(2)}, u32[]{:S(2)}) collective-permute-start(f32[8,5,4,128]{3,2,1,0:T(4,128)S(1)} %get-tuple-element.23.own_ref), channel_id=1, source_target_pairs={{0,1},{1,0},{2,3},{3,2},{4,5},{5,4},{6,7},{7,6},{8,9},{9,8},{10,11... | collective-permute-start | bytes 245768 | tf_op jit(solution)/shard_map/ppermute | solution.py:349
  45.4 44.3 %copy-start.1 = (f32[3,512]{1,0:T(4,128)S(1)}, f32[3,512]{1,0:T(4,128)}, u32[]{:S(2)}) copy-start(f32[3,512]{1,0:T(4,128)} %vel_ref.1) | copy-start | bytes 18436
  60.2 11.2 %all-to-all-start.2 = ((f32[16,2,3,4,128]{4,3,2,1,0:T(4,128)}), f32[16,2,3,4,128]{4,3,2,1,0:T(4,128)S(1)}, u32[]{:S(2)}, u32[]{:S(2)}) async-start(f32[16,2,3,4,128]{4,3,2,1,0:T(4,128)} %bitcast.7), calls=%async_computation.2 | async-start | bytes 393216 | tf_op jit(solution)/shard_map/all_to_all | solution.py:385
  64.8 3.1 %collective-permute-start.1 = (f32[8,3,4,128]{3,2,1,0:T(4,128)S(1)}, f32[8,3,4,128]{3,2,1,0:T(4,128)S(1)}, u32[]{:S(2)}, u32[]{:S(2)}) collective-permute-start(f32[8,3,4,128]{3,2,1,0:T(4,128)S(1)} %get-tuple-element.29), channel_id=1, source_target_pairs={{0,1},{1,0},{2,3},{3,2},{4,5},{5,4},{6,7},{7,6},{8,9},{9,8},{10,11... | collective-permute-start | bytes 147464 | tf_op jit(solution)/shard_map/ppermute | solution.py:384

commit v6 on v5

--- a/solution.py
+++ b/solution.py
@@ -1,4 +1,3 @@
-import functools
 import jax
 import jax.numpy as jnp
 from jax import lax
@@ -27,6 +26,7 @@
 CHANNELS = 5
 TYPE_ROWS = 24
 UNROLL = 16
+LAG = 8
 PREPARED = 32
 
 def split_three(values):
@@ -187,9 +187,8 @@
         coulomb = charge * (inverse * root - 2.0 * REACTION)
         switch = jnp.maximum((CUT_SQ + SOFT_CORE) - soft_sq, 0.0)
         scalar = (dispersion + coulomb) * (switch * switch)
-        if same is not None:
-            at_i = lax.broadcasted_iota(jnp.int32, (TILE_ATOMS, LANES), 0)
-            scalar = jnp.where((at_i < lane) | jnp.logical_not(same), scalar, 0.0)
+        at_i = lax.broadcasted_iota(jnp.int32, (TILE_ATOMS, LANES), 0)
+        scalar = jnp.where((at_i < lane) | jnp.logical_not(same), scalar, 0.0)
         high = scalar.astype(bf16)
         scalar_ref[part, 0] = high
         scalar_ref[part, 1] = (scalar - high.astype(f32)).astype(bf16)
@@ -231,31 +230,23 @@
 
     def step(index, before):
         found = [find(index * UNROLL + part) for part in range(UNROLL)]
-        any_same = functools.reduce(jnp.logical_or, [same for _, _, same in found])
-
-        def work(masked):
+        for start in range(0, UNROLL, LAG):
             looked = []
-            for part, (first, place, _) in enumerate(found):
-                looked.append(features(first, place))
-                add_forces(before[2 * part], before[2 * part + 1], part)
-            for part, (_, _, same) in enumerate(found):
-                scalars(looked[part], same if masked else None, part)
-
-        @pl.when(any_same)
-        def _():
-            work(True)
-
-        @pl.when(jnp.logical_not(any_same))
-        def _():
-            work(False)
-
-        return tuple(place for first, second, _ in found for place in (first, second))
+            for part in range(start, start + LAG):
+                looked.append(features(*found[part][:2]))
+                if part < LAG:
+                    add_forces(before[2 * part], before[2 * part + 1], UNROLL - LAG + part)
+                else:
+                    add_forces(*found[part - LAG][:2], part - LAG)
+            for part in range(start, start + LAG):
+                scalars(looked[part - start], found[part][2], part)
+        return tuple(place for first, second, _ in found[-LAG:] for place in (first, second))
 
     last = lax.fori_loop(
-        0, pairs_ref[2, 0] // UNROLL, step, tuple(jnp.int32(0) for _ in range(2 * UNROLL))
-    )
-    for part in range(UNROLL):
-        add_forces(last[2 * part], last[2 * part + 1], part)
+        0, pairs_ref[2, 0] // UNROLL, step, tuple(jnp.int32(0) for _ in range(2 * LAG))
+    )
+    for part in range(LAG):
+        add_forces(last[2 * part], last[2 * part + 1], UNROLL - LAG + part)
 
     def gather_owners(index, carry):
         for source, start, target in (

time: 91.1 us -> 89.6 us (0.984)
  the two profiles are of different devices: /device:TPU:2 before, /device:TPU:32 now
where the time goes in v6:
time: 89.6 us; the launch traced here: 88.8 us
  starting transfers between devices  29.6 us (33%)
  waiting for transfers between devices  23.4 us (26%)
  blocking collectives  17.5 us (20%)
  Pallas kernels  13.5 us (15%)
  local copies, waits for them, and re-layouts  2.54 us (3%)
  between operations  1.38 us (2%)
    all_to_all x1, blocking collectives, shards(): lax.all_to_all(jnp.where(to_zh == my_zh, row_sum[None], far_sum).reshape(...  17.5 us
    all_to_all x1, starting transfers between devices, shards(): lax.all_to_all(blocks, ('row', 'col'), 0, 0, axis_index_groups=z_groups)  15.2 us
    all_to_all x1, waiting for transfers between devices, shards(): lax.all_to_all(blocks, ('row', 'col'), 0, 0, axis_index_groups=z_groups)  11.8 us
    pallas_call x1, Pallas kernels, shards(): pl.pallas_call(pair_kernel, out_shape=(jax.ShapeDtypeStruct((n_zl, 3, til...  10.1 us
    all_to_all x1, starting transfers between devices, shards(): col_blocks = lax.all_to_all(both, 'row', 0, 0, axis_index_groups=xy_groups)  7.03 us
    all_to_all x1, waiting for transfers between devices, shards(): lax.all_to_all(col_force.reshape(n_xy, ZH_SIZE, 3, tiles_dev, LANES), 'ro...  4.89 us
    all_to_all x1, waiting for transfers between devices, shards(): col_blocks = lax.all_to_all(both, 'row', 0, 0, axis_index_groups=xy_groups)  4.5 us
    all_to_all x1, starting transfers between devices, shards(): lax.all_to_all(col_force.reshape(n_xy, ZH_SIZE, 3, tiles_dev, LANES), 'ro...  3.52 us
  transfers between devices with their start and end apart: 5, of which 5 were waited for; matrix products, arithmetic and copies ran while one was open for 2% of the time, Pallas kernels for 1%

profile of v6, /device:TPU:32, one launch (start us, length us, event | category | flops | bytes accessed | tf_op | source)
XLA Modules:
  0.0 88.8 jit_solution(8353355227187384132)
XLA Ops:
  0.6 1.4 %pack_atoms.1 = (f32[3,512]{1,0:T(4,128)}, f32[16,5,4,128]{3,2,1,0:T(4,128)}) custom-call(f32[3,512]{1,0:T(4,128)} %positions_ref.1, f32[3,512]{1,0:T(4,128)} %vel_ref.1, f32[4,128]{1,0:T(4,128)} %bitcast.26, s32[4,128]{1,0:T(4,128)} %bitcast.27), custom_call_target="tpu_custom_call" | custom-call | tf_op jit(solution)/shard_map/pack_atoms/pallas_call | solution.py:294
  2.0 15.2 %all-to-all-start = ((f32[16,5,4,128]{3,2,1,0:T(4,128)}), f32[16,5,4,128]{3,2,1,0:T(4,128)S(1)}, u32[]{:S(2)}, u32[]{:S(2)}) async-start(f32[16,5,4,128]{3,2,1,0:T(4,128)} %get-tuple-element.18), calls=%async_computation | async-start | bytes 327680 | tf_op jit(solution)/shard_map/all_to_all | solution.py:326
  17.9 0.8 copy.16
  18.7 0.8 copy.17
  19.5 0.0 copy-start
  19.5 0.7 copy-done
  20.2 0.1 tables.1
  20.3 11.8 %all-to-all-done.z_ref = f32[16,5,4,128]{3,2,1,0:T(4,128)S(1)} async-done(((f32[16,5,4,128]{3,2,1,0:T(4,128)}), f32[16,5,4,128]{3,2,1,0:T(4,128)S(1)}, u32[]{:S(2)}, u32[]{:S(2)}) %all-to-all-start) | async-done | bytes 163872 | tf_op jit(solution)/shard_map/all_to_all | solution.py:326
  32.1 0.8 join_halves.1
  32.9 7.0 %all-to-all-start.1 = ((f32[16,2,5,4,128]{4,3,2,1,0:T(4,128)}), f32[16,2,5,4,128]{4,3,2,1,0:T(4,128)S(1)}, u32[]{:S(2)}, u32[]{:S(2)}) async-start(f32[16,2,5,4,128]{4,3,2,1,0:T(4,128)} %get-tuple-element.27), calls=%async_computation.1 | async-start | bytes 655360 | tf_op jit(solution)/shard_map/all_to_all | solution.py:339
  39.9 1.9 %collective-permute-start = (f32[8,5,4,128]{3,2,1,0:T(4,128)S(1)}, f32[8,5,4,128]{3,2,1,0:T(4,128)S(1)}, u32[]{:S(2)}, u32[]{:S(2)}) collective-permute-start(f32[8,5,4,128]{3,2,1,0:T(4,128)S(1)} %get-tuple-element.23.own_ref), channel_id=1, source_target_pairs={{0,1},{1,0},{2,3},{3,2},{4,5},{5,4},{6,7},{7,6},{8,9},{9,8},{10,11... | collective-permute-start | bytes 245768 | tf_op jit(solution)/shard_map/ppermute | solution.py:340
  41.9 1.2 %collective-permute-done.other_ref = f32[8,5,4,128]{3,2,1,0:T(4,128)S(1)} collective-permute-done((f32[8,5,4,128]{3,2,1,0:T(4,128)S(1)}, f32[8,5,4,128]{3,2,1,0:T(4,128)S(1)}, u32[]{:S(2)}, u32[]{:S(2)}) %collective-permute-start) | collective-permute-done | bytes 81952 | tf_op jit(solution)/shard_map/ppermute | solution.py:340
  43.1 1.1 %row_factors.1 = (f32[64,8,128]{2,1,0:T(8,128)S(1)}, bf16[64,128,128]{2,1,0:T(8,128)(2,1)S(1)}) custom-call(f32[8,5,4,128]{3,2,1,0:T(4,128)S(1)} %get-tuple-element.23.own_ref, f32[8,5,4,128]{3,2,1,0:T(4,128)S(1)} %collective-permute-done.other_ref, bf16[96,24]{1,0:T(8,128)(2,1)S(1)} %get-tuple-element.24.table_ref), custom_call_target="tpu_custom_call" | custom-call | flops 201326592 | bytes 4194304 | tf_op jit(solution)/shard_map/row_factors/pallas_call | solution.py:343
  44.2 0.0 copy-start.1
  44.3 4.5 %all-to-all-done.1 = f32[16,2,5,4,128]{4,3,2,1,0:T(4,128)S(1)} async-done(((f32[16,2,5,4,128]{4,3,2,1,0:T(4,128)}), f32[16,2,5,4,128]{4,3,2,1,0:T(4,128)S(1)}, u32[]{:S(2)}, u32[]{:S(2)}) %all-to-all-start.1) | async-done | bytes 327712 | tf_op jit(solution)/shard_map/all_to_all | solution.py:339
  48.8 10.1 %pair_forces.1 = (f32[8,3,4,128]{3,2,1,0:T(4,128)S(1)}, f32[8,3,4,128]{3,2,1,0:T(4,128)S(1)}, f32[4,8,3,4,128]{4,3,2,1,0:T(4,128)}) custom-call(s32[3,128]{1,0:T(4,128)S(1)} %get-tuple-element.21.pairs_ref, f32[64,8,128]{2,1,0:T(8,128)S(1)} %get-tuple-element.25.row_block, bf16[64,128,128]{2,1,0:T(8,128)(2,1)S(1)} %get-tuple-element.26.lhs_ref, ...), custom_call_target="tpu_custom_call" | custom-call | tf_op jit(solution)/shard_map/pair_forces/pallas_call | solution.py:357
  58.9 3.5 %all-to-all-start.2 = ((f32[16,2,3,4,128]{4,3,2,1,0:T(4,128)}), f32[16,2,3,4,128]{4,3,2,1,0:T(4,128)S(1)}, u32[]{:S(2)}, u32[]{:S(2)}) async-start(f32[16,2,3,4,128]{4,3,2,1,0:T(4,128)} %bitcast.7), calls=%async_computation.2 | async-start | bytes 393216 | tf_op jit(solution)/shard_map/all_to_all | solution.py:376
  62.4 1.9 %collective-permute-start.1 = (f32[8,3,4,128]{3,2,1,0:T(4,128)S(1)}, f32[8,3,4,128]{3,2,1,0:T(4,128)S(1)}, u32[]{:S(2)}, u32[]{:S(2)}) collective-permute-start(f32[8,3,4,128]{3,2,1,0:T(4,128)S(1)} %get-tuple-element.29), channel_id=1, source_target_pairs={{0,1},{1,0},{2,3},{3,2},{4,5},{5,4},{6,7},{7,6},{8,9},{9,8},{10,11... | collective-permute-start | bytes 147464 | tf_op jit(solution)/shard_map/ppermute | solution.py:375
  64.4 0.1 iota.21
  64.5 0.1 iota.22
  64.6 0.1 iota.26
  64.6 0.9 %collective-permute-done.1 = f32[8,3,4,128]{3,2,1,0:T(4,128)S(1)} collective-permute-done((f32[8,3,4,128]{3,2,1,0:T(4,128)S(1)}, f32[8,3,4,128]{3,2,1,0:T(4,128)S(1)}, u32[]{:S(2)}, u32[]{:S(2)}) %collective-permute-start.1) | collective-permute-done | bytes 49184 | tf_op jit(solution)/shard_map/ppermute | solution.py:375
  65.6 4.9 %all-to-all-done.2 = f32[16,2,3,4,128]{4,3,2,1,0:T(4,128)S(1)} async-done(((f32[16,2,3,4,128]{4,3,2,1,0:T(4,128)}), f32[16,2,3,4,128]{4,3,2,1,0:T(4,128)S(1)}, u32[]{:S(2)}, u32[]{:S(2)}) %all-to-all-start.2) | async-done | bytes 196640 | tf_op jit(solution)/shard_map/all_to_all | solution.py:376
  70.5 0.1 bitcast_select_fusion
  70.6 17.5 %all_to_all.20 = f32[16,3,4,128]{3,2,1,0:T(4,128)S(1)} all-to-all(f32[16,3,4,128]{3,2,1,0:T(4,128)S(1)} %bitcast_select_fusion), channel_id=1, replica_groups={{0,2,4,6,8,10,12,14,64,66,68,70,72,74,76,78},{1,3,5,7,9,11,13,15,65,67,..., dimensions={0} | all-to-all | bytes 196608 | tf_op jit(solution)/shard_map/all_to_all | solution.py:388
  88.2 0.0 copy-done.1
  88.2 0.6 multiply_add_fusion
  (9 shorter events, 0.1 us)
Async XLA Ops:
  2.0 30.1 %all-to-all-start = ((f32[16,5,4,128]{3,2,1,0:T(4,128)}), f32[16,5,4,128]{3,2,1,0:T(4,128)S(1)}, u32[]{:S(2)}, u32[]{:S(2)}) async-start(f32[16,5,4,128]{3,2,1,0:T(4,128)} %get-tuple-element.18), calls=%async_computation | async-start | bytes 327680 | tf_op jit(solution)/shard_map/all_to_all | solution.py:326
  19.5 0.7 copy-start
  32.9 15.9 %all-to-all-start.1 = ((f32[16,2,5,4,128]{4,3,2,1,0:T(4,128)}), f32[16,2,5,4,128]{4,3,2,1,0:T(4,128)S(1)}, u32[]{:S(2)}, u32[]{:S(2)}) async-start(f32[16,2,5,4,128]{4,3,2,1,0:T(4,128)} %get-tuple-element.27), calls=%async_computation.1 | async-start | bytes 655360 | tf_op jit(solution)/shard_map/all_to_all | solution.py:339
  39.9 3.2 %collective-permute-start = (f32[8,5,4,128]{3,2,1,0:T(4,128)S(1)}, f32[8,5,4,128]{3,2,1,0:T(4,128)S(1)}, u32[]{:S(2)}, u32[]{:S(2)}) collective-permute-start(f32[8,5,4,128]{3,2,1,0:T(4,128)S(1)} %get-tuple-element.23.own_ref), channel_id=1, source_target_pairs={{0,1},{1,0},{2,3},{3,2},{4,5},{5,4},{6,7},{7,6},{8,9},{9,8},{10,11... | collective-permute-start | bytes 245768 | tf_op jit(solution)/shard_map/ppermute | solution.py:340
  44.2 43.9 %copy-start.1 = (f32[3,512]{1,0:T(4,128)S(1)}, f32[3,512]{1,0:T(4,128)}, u32[]{:S(2)}) copy-start(f32[3,512]{1,0:T(4,128)} %vel_ref.1) | copy-start | bytes 18436
  58.9 11.6 %all-to-all-start.2 = ((f32[16,2,3,4,128]{4,3,2,1,0:T(4,128)}), f32[16,2,3,4,128]{4,3,2,1,0:T(4,128)S(1)}, u32[]{:S(2)}, u32[]{:S(2)}) async-start(f32[16,2,3,4,128]{4,3,2,1,0:T(4,128)} %bitcast.7), calls=%async_computation.2 | async-start | bytes 393216 | tf_op jit(solution)/shard_map/all_to_all | solution.py:376
  62.4 3.1 %collective-permute-start.1 = (f32[8,3,4,128]{3,2,1,0:T(4,128)S(1)}, f32[8,3,4,128]{3,2,1,0:T(4,128)S(1)}, u32[]{:S(2)}, u32[]{:S(2)}) collective-permute-start(f32[8,3,4,128]{3,2,1,0:T(4,128)S(1)} %get-tuple-element.29), channel_id=1, source_target_pairs={{0,1},{1,0},{2,3},{3,2},{4,5},{5,4},{6,7},{7,6},{8,9},{9,8},{10,11... | collective-permute-start | bytes 147464 | tf_op jit(solution)/shard_map/ppermute | solution.py:375

commit v7 on v6

--- a/solution.py
+++ b/solution.py
@@ -141,11 +141,12 @@
     bf16 = jnp.bfloat16
     sub8 = lax.broadcasted_iota(jnp.int32, (8, LANES), 0)
     sub8 = lax.broadcasted_iota(jnp.int32, (8, LANES), 0)
-    lane = lax.broadcasted_iota(jnp.int32, (TILE_ATOMS, LANES), 1)
+    shape = (TILE_ATOMS, LANES)
+    ahead = lax.broadcasted_iota(jnp.int32, shape, 1) - lax.broadcasted_iota(jnp.int32, shape, 0)
 
     row_sum[...] = jnp.zeros(row_sum.shape, f32)
     col_sum[...] = jnp.zeros(col_sum.shape, f32)
-    scalar_ref[...] = jnp.zeros(scalar_ref.shape, bf16)
+    scalar_ref[UNROLL - LAG :] = jnp.zeros((LAG, *scalar_ref.shape[1:]), bf16)
 
     def spread_owners(index, carry):
         for part in range(4):
@@ -187,8 +188,8 @@
         coulomb = charge * (inverse * root - 2.0 * REACTION)
         switch = jnp.maximum((CUT_SQ + SOFT_CORE) - soft_sq, 0.0)
         scalar = (dispersion + coulomb) * (switch * switch)
-        at_i = lax.broadcasted_iota(jnp.int32, (TILE_ATOMS, LANES), 0)
-        scalar = jnp.where((at_i < lane) | jnp.logical_not(same), scalar, 0.0)
+        least = jnp.where(same, 1, -TILE_ATOMS)
+        scalar = jnp.where(ahead >= least, scalar, 0.0)
         high = scalar.astype(bf16)
         scalar_ref[part, 0] = high
         scalar_ref[part, 1] = (scalar - high.astype(f32)).astype(bf16)

time: 89.6 us -> 89.4 us (level)
  starting transfers between devices: 29.6 us -> 33.7 us
  Pallas kernels: 13.5 us -> 9.58 us
    all_to_all x1, starting transfers between devices: 3.52 us -> 7.61 us  [shards(): lax.all_to_all(col_force.reshape(n_xy, ZH_SIZE, 3, tiles_dev, LANES), 'ro...]
    pallas_call x1, Pallas kernels: 10.1 us -> 6.18 us  [shards(): pl.pallas_call(pair_kernel, out_shape=(jax.ShapeDtypeStruct((n_zl, 3, til...]
where the time goes in v7:
time: 89.4 us; the launch traced here: 88.6 us
  starting transfers between devices  33.7 us (38%)
  waiting for transfers between devices  23.4 us (26%)
  blocking collectives  17.1 us (19%)
  Pallas kernels  9.58 us (11%)
  local copies, waits for them, and re-layouts  2.54 us (3%)
  between operations  1.38 us (2%)
    all_to_all x1, blocking collectives, shards(): lax.all_to_all(jnp.where(to_zh == my_zh, row_sum[None], far_sum).reshape(...  17.1 us
    all_to_all x1, starting transfers between devices, shards(): lax.all_to_all(blocks, ('row', 'col'), 0, 0, axis_index_groups=z_groups)  15.2 us
    all_to_all x1, waiting for transfers between devices, shards(): lax.all_to_all(blocks, ('row', 'col'), 0, 0, axis_index_groups=z_groups)  11.8 us
    all_to_all x1, starting transfers between devices, shards(): lax.all_to_all(col_force.reshape(n_xy, ZH_SIZE, 3, tiles_dev, LANES), 'ro...  7.61 us
    all_to_all x1, starting transfers between devices, shards(): col_blocks = lax.all_to_all(both, 'row', 0, 0, axis_index_groups=xy_groups)  7.03 us
    pallas_call x1, Pallas kernels, shards(): pl.pallas_call(pair_kernel, out_shape=(jax.ShapeDtypeStruct((n_zl, 3, til...  6.18 us
    all_to_all x1, waiting for transfers between devices, shards(): lax.all_to_all(col_force.reshape(n_xy, ZH_SIZE, 3, tiles_dev, LANES), 'ro...  4.92 us
    all_to_all x1, waiting for transfers between devices, shards(): col_blocks = lax.all_to_all(both, 'row', 0, 0, axis_index_groups=xy_groups)  4.5 us
  transfers between devices with their start and end apart: 5, of which 5 were waited for; matrix products, arithmetic and copies ran while one was open for 2% of the time, Pallas kernels for 1%

profile of v7, /device:TPU:32, one launch (start us, length us, event | category | flops | bytes accessed | tf_op | source)
XLA Modules:
  0.0 88.6 jit_solution(7953418056706010022)
XLA Ops:
  0.6 1.4 %pack_atoms.1 = (f32[3,512]{1,0:T(4,128)}, f32[16,5,4,128]{3,2,1,0:T(4,128)}) custom-call(f32[3,512]{1,0:T(4,128)} %positions_ref.1, f32[3,512]{1,0:T(4,128)} %vel_ref.1, f32[4,128]{1,0:T(4,128)} %bitcast.26, s32[4,128]{1,0:T(4,128)} %bitcast.27), custom_call_target="tpu_custom_call" | custom-call | tf_op jit(solution)/shard_map/pack_atoms/pallas_call | solution.py:295
  2.0 15.2 %all-to-all-start = ((f32[16,5,4,128]{3,2,1,0:T(4,128)}), f32[16,5,4,128]{3,2,1,0:T(4,128)S(1)}, u32[]{:S(2)}, u32[]{:S(2)}) async-start(f32[16,5,4,128]{3,2,1,0:T(4,128)} %get-tuple-element.18), calls=%async_computation | async-start | bytes 327680 | tf_op jit(solution)/shard_map/all_to_all | solution.py:327
  17.9 0.8 copy.16
  18.7 0.8 copy.17
  19.5 0.0 copy-start
  19.5 0.7 copy-done
  20.2 0.1 tables.1
  20.3 11.8 %all-to-all-done.z_ref = f32[16,5,4,128]{3,2,1,0:T(4,128)S(1)} async-done(((f32[16,5,4,128]{3,2,1,0:T(4,128)}), f32[16,5,4,128]{3,2,1,0:T(4,128)S(1)}, u32[]{:S(2)}, u32[]{:S(2)}) %all-to-all-start) | async-done | bytes 163872 | tf_op jit(solution)/shard_map/all_to_all | solution.py:327
  32.1 0.8 join_halves.1
  32.9 7.0 %all-to-all-start.1 = ((f32[16,2,5,4,128]{4,3,2,1,0:T(4,128)}), f32[16,2,5,4,128]{4,3,2,1,0:T(4,128)S(1)}, u32[]{:S(2)}, u32[]{:S(2)}) async-start(f32[16,2,5,4,128]{4,3,2,1,0:T(4,128)} %get-tuple-element.27), calls=%async_computation.1 | async-start | bytes 655360 | tf_op jit(solution)/shard_map/all_to_all | solution.py:340
  39.9 1.9 %collective-permute-start = (f32[8,5,4,128]{3,2,1,0:T(4,128)S(1)}, f32[8,5,4,128]{3,2,1,0:T(4,128)S(1)}, u32[]{:S(2)}, u32[]{:S(2)}) collective-permute-start(f32[8,5,4,128]{3,2,1,0:T(4,128)S(1)} %get-tuple-element.23.own_ref), channel_id=1, source_target_pairs={{0,1},{1,0},{2,3},{3,2},{4,5},{5,4},{6,7},{7,6},{8,9},{9,8},{10,11... | collective-permute-start | bytes 245768 | tf_op jit(solution)/shard_map/ppermute | solution.py:341
  41.9 1.2 %collective-permute-done.other_ref = f32[8,5,4,128]{3,2,1,0:T(4,128)S(1)} collective-permute-done((f32[8,5,4,128]{3,2,1,0:T(4,128)S(1)}, f32[8,5,4,128]{3,2,1,0:T(4,128)S(1)}, u32[]{:S(2)}, u32[]{:S(2)}) %collective-permute-start) | collective-permute-done | bytes 81952 | tf_op jit(solution)/shard_map/ppermute | solution.py:341
  43.1 1.1 %row_factors.1 = (f32[64,8,128]{2,1,0:T(8,128)S(1)}, bf16[64,128,128]{2,1,0:T(8,128)(2,1)S(1)}) custom-call(f32[8,5,4,128]{3,2,1,0:T(4,128)S(1)} %get-tuple-element.23.own_ref, f32[8,5,4,128]{3,2,1,0:T(4,128)S(1)} %collective-permute-done.other_ref, bf16[96,24]{1,0:T(8,128)(2,1)S(1)} %get-tuple-element.24.table_ref), custom_call_target="tpu_custom_call" | custom-call | flops 201326592 | bytes 4194304 | tf_op jit(solution)/shard_map/row_factors/pallas_call | solution.py:344
  44.2 0.0 copy-start.1
  44.3 4.5 %all-to-all-done.1 = f32[16,2,5,4,128]{4,3,2,1,0:T(4,128)S(1)} async-done(((f32[16,2,5,4,128]{4,3,2,1,0:T(4,128)}), f32[16,2,5,4,128]{4,3,2,1,0:T(4,128)S(1)}, u32[]{:S(2)}, u32[]{:S(2)}) %all-to-all-start.1) | async-done | bytes 327712 | tf_op jit(solution)/shard_map/all_to_all | solution.py:340
  48.8 6.2 %pair_forces.1 = (f32[8,3,4,128]{3,2,1,0:T(4,128)S(1)}, f32[8,3,4,128]{3,2,1,0:T(4,128)S(1)}, f32[4,8,3,4,128]{4,3,2,1,0:T(4,128)}) custom-call(s32[3,128]{1,0:T(4,128)S(1)} %get-tuple-element.21.pairs_ref, f32[64,8,128]{2,1,0:T(8,128)S(1)} %get-tuple-element.25.row_block, bf16[64,128,128]{2,1,0:T(8,128)(2,1)S(1)} %get-tuple-element.26.lhs_ref, ...), custom_call_target="tpu_custom_call" | custom-call | tf_op jit(solution)/shard_map/pair_forces/pallas_call | solution.py:358
  54.9 7.6 %all-to-all-start.2 = ((f32[16,2,3,4,128]{4,3,2,1,0:T(4,128)}), f32[16,2,3,4,128]{4,3,2,1,0:T(4,128)S(1)}, u32[]{:S(2)}, u32[]{:S(2)}) async-start(f32[16,2,3,4,128]{4,3,2,1,0:T(4,128)} %bitcast.7), calls=%async_computation.2 | async-start | bytes 393216 | tf_op jit(solution)/shard_map/all_to_all | solution.py:377
  62.6 1.9 %collective-permute-start.1 = (f32[8,3,4,128]{3,2,1,0:T(4,128)S(1)}, f32[8,3,4,128]{3,2,1,0:T(4,128)S(1)}, u32[]{:S(2)}, u32[]{:S(2)}) collective-permute-start(f32[8,3,4,128]{3,2,1,0:T(4,128)S(1)} %get-tuple-element.29), channel_id=1, source_target_pairs={{0,1},{1,0},{2,3},{3,2},{4,5},{5,4},{6,7},{7,6},{8,9},{9,8},{10,11... | collective-permute-start | bytes 147464 | tf_op jit(solution)/shard_map/ppermute | solution.py:376
  64.5 0.1 iota.21
  64.6 0.1 iota.22
  64.7 0.1 iota.26
  64.8 0.9 %collective-permute-done.1 = f32[8,3,4,128]{3,2,1,0:T(4,128)S(1)} collective-permute-done((f32[8,3,4,128]{3,2,1,0:T(4,128)S(1)}, f32[8,3,4,128]{3,2,1,0:T(4,128)S(1)}, u32[]{:S(2)}, u32[]{:S(2)}) %collective-permute-start.1) | collective-permute-done | bytes 49184 | tf_op jit(solution)/shard_map/ppermute | solution.py:376
  65.7 4.9 %all-to-all-done.2 = f32[16,2,3,4,128]{4,3,2,1,0:T(4,128)S(1)} async-done(((f32[16,2,3,4,128]{4,3,2,1,0:T(4,128)}), f32[16,2,3,4,128]{4,3,2,1,0:T(4,128)S(1)}, u32[]{:S(2)}, u32[]{:S(2)}) %all-to-all-start.2) | async-done | bytes 196640 | tf_op jit(solution)/shard_map/all_to_all | solution.py:377
  70.7 0.1 bitcast_select_fusion
  70.8 17.1 %all_to_all.20 = f32[16,3,4,128]{3,2,1,0:T(4,128)S(1)} all-to-all(f32[16,3,4,128]{3,2,1,0:T(4,128)S(1)} %bitcast_select_fusion), channel_id=1, replica_groups={{0,2,4,6,8,10,12,14,64,66,68,70,72,74,76,78},{1,3,5,7,9,11,13,15,65,67,..., dimensions={0} | all-to-all | bytes 196608 | tf_op jit(solution)/shard_map/all_to_all | solution.py:389
  88.0 0.0 copy-done.1
  88.0 0.6 multiply_add_fusion
  (9 shorter events, 0.1 us)
Async XLA Ops:
  2.0 30.1 %all-to-all-start = ((f32[16,5,4,128]{3,2,1,0:T(4,128)}), f32[16,5,4,128]{3,2,1,0:T(4,128)S(1)}, u32[]{:S(2)}, u32[]{:S(2)}) async-start(f32[16,5,4,128]{3,2,1,0:T(4,128)} %get-tuple-element.18), calls=%async_computation | async-start | bytes 327680 | tf_op jit(solution)/shard_map/all_to_all | solution.py:327
  19.5 0.7 copy-start
  32.9 15.9 %all-to-all-start.1 = ((f32[16,2,5,4,128]{4,3,2,1,0:T(4,128)}), f32[16,2,5,4,128]{4,3,2,1,0:T(4,128)S(1)}, u32[]{:S(2)}, u32[]{:S(2)}) async-start(f32[16,2,5,4,128]{4,3,2,1,0:T(4,128)} %get-tuple-element.27), calls=%async_computation.1 | async-start | bytes 655360 | tf_op jit(solution)/shard_map/all_to_all | solution.py:340
  39.9 3.2 %collective-permute-start = (f32[8,5,4,128]{3,2,1,0:T(4,128)S(1)}, f32[8,5,4,128]{3,2,1,0:T(4,128)S(1)}, u32[]{:S(2)}, u32[]{:S(2)}) collective-permute-start(f32[8,5,4,128]{3,2,1,0:T(4,128)S(1)} %get-tuple-element.23.own_ref), channel_id=1, source_target_pairs={{0,1},{1,0},{2,3},{3,2},{4,5},{5,4},{6,7},{7,6},{8,9},{9,8},{10,11... | collective-permute-start | bytes 245768 | tf_op jit(solution)/shard_map/ppermute | solution.py:341
  44.2 43.7 %copy-start.1 = (f32[3,512]{1,0:T(4,128)S(1)}, f32[3,512]{1,0:T(4,128)}, u32[]{:S(2)}) copy-start(f32[3,512]{1,0:T(4,128)} %vel_ref.1) | copy-start | bytes 18436
  54.9 15.7 %all-to-all-start.2 = ((f32[16,2,3,4,128]{4,3,2,1,0:T(4,128)}), f32[16,2,3,4,128]{4,3,2,1,0:T(4,128)S(1)}, u32[]{:S(2)}, u32[]{:S(2)}) async-start(f32[16,2,3,4,128]{4,3,2,1,0:T(4,128)} %bitcast.7), calls=%async_computation.2 | async-start | bytes 393216 | tf_op jit(solution)/shard_map/all_to_all | solution.py:377
  62.6 3.1 %collective-permute-start.1 = (f32[8,3,4,128]{3,2,1,0:T(4,128)S(1)}, f32[8,3,4,128]{3,2,1,0:T(4,128)S(1)}, u32[]{:S(2)}, u32[]{:S(2)}) collective-permute-start(f32[8,3,4,128]{3,2,1,0:T(4,128)S(1)} %get-tuple-element.29), channel_id=1, source_target_pairs={{0,1},{1,0},{2,3},{3,2},{4,5},{5,4},{6,7},{7,6},{8,9},{9,8},{10,11... | collective-permute-start | bytes 147464 | tf_op jit(solution)/shard_map/ppermute | solution.py:376

commit v8 on v7

--- a/solution.py
+++ b/solution.py
@@ -26,7 +26,7 @@
 CHANNELS = 5
 TYPE_ROWS = 24
 UNROLL = 16
-LAG = 8
+LAG = 4
 PREPARED = 32
 
 def split_three(values):

time: 89.4 us -> 89.1 us (level)
  no operation moved by 1% of the time
where the time goes in v8:
time: 89.1 us; the launch traced here: 88.4 us
  starting transfers between devices  33.7 us (38%)
  waiting for transfers between devices  23.4 us (26%)
  blocking collectives  17.1 us (19%)
  Pallas kernels  9.4 us (11%)
  local copies, waits for them, and re-layouts  2.54 us (3%)
  between operations  1.38 us (2%)
    all_to_all x1, blocking collectives, shards(): lax.all_to_all(jnp.where(to_zh == my_zh, row_sum[None], far_sum).reshape(...  17.1 us
    all_to_all x1, starting transfers between devices, shards(): lax.all_to_all(blocks, ('row', 'col'), 0, 0, axis_index_groups=z_groups)  15.2 us
    all_to_all x1, waiting for transfers between devices, shards(): lax.all_to_all(blocks, ('row', 'col'), 0, 0, axis_index_groups=z_groups)  11.8 us
    all_to_all x1, starting transfers between devices, shards(): lax.all_to_all(col_force.reshape(n_xy, ZH_SIZE, 3, tiles_dev, LANES), 'ro...  7.59 us
    all_to_all x1, starting transfers between devices, shards(): col_blocks = lax.all_to_all(both, 'row', 0, 0, axis_index_groups=xy_groups)  7.03 us
    pallas_call x1, Pallas kernels, shards(): pl.pallas_call(pair_kernel, out_shape=(jax.ShapeDtypeStruct((n_zl, 3, til...  6 us
    all_to_all x1, waiting for transfers between devices, shards(): lax.all_to_all(col_force.reshape(n_xy, ZH_SIZE, 3, tiles_dev, LANES), 'ro...  4.92 us
    all_to_all x1, waiting for transfers between devices, shards(): col_blocks = lax.all_to_all(both, 'row', 0, 0, axis_index_groups=xy_groups)  4.5 us
  transfers between devices with their start and end apart: 5, of which 5 were waited for; matrix products, arithmetic and copies ran while one was open for 2% of the time, Pallas kernels for 1%

profile of v8, /device:TPU:32, one launch (start us, length us, event | category | flops | bytes accessed | tf_op | source)
XLA Modules:
  0.0 88.4 jit_solution(7792315790131800500)
XLA Ops:
  0.6 1.4 %pack_atoms.1 = (f32[3,512]{1,0:T(4,128)}, f32[16,5,4,128]{3,2,1,0:T(4,128)}) custom-call(f32[3,512]{1,0:T(4,128)} %positions_ref.1, f32[3,512]{1,0:T(4,128)} %vel_ref.1, f32[4,128]{1,0:T(4,128)} %bitcast.26, s32[4,128]{1,0:T(4,128)} %bitcast.27), custom_call_target="tpu_custom_call" | custom-call | tf_op jit(solution)/shard_map/pack_atoms/pallas_call | solution.py:295
  2.0 15.2 %all-to-all-start = ((f32[16,5,4,128]{3,2,1,0:T(4,128)}), f32[16,5,4,128]{3,2,1,0:T(4,128)S(1)}, u32[]{:S(2)}, u32[]{:S(2)}) async-start(f32[16,5,4,128]{3,2,1,0:T(4,128)} %get-tuple-element.18), calls=%async_computation | async-start | bytes 327680 | tf_op jit(solution)/shard_map/all_to_all | solution.py:327
  17.9 0.8 copy.16
  18.7 0.8 copy.17
  19.5 0.0 copy-start
  19.5 0.7 copy-done
  20.2 0.1 tables.1
  20.3 11.8 %all-to-all-done.z_ref = f32[16,5,4,128]{3,2,1,0:T(4,128)S(1)} async-done(((f32[16,5,4,128]{3,2,1,0:T(4,128)}), f32[16,5,4,128]{3,2,1,0:T(4,128)S(1)}, u32[]{:S(2)}, u32[]{:S(2)}) %all-to-all-start) | async-done | bytes 163872 | tf_op jit(solution)/shard_map/all_to_all | solution.py:327
  32.1 0.8 join_halves.1
  32.9 7.0 %all-to-all-start.1 = ((f32[16,2,5,4,128]{4,3,2,1,0:T(4,128)}), f32[16,2,5,4,128]{4,3,2,1,0:T(4,128)S(1)}, u32[]{:S(2)}, u32[]{:S(2)}) async-start(f32[16,2,5,4,128]{4,3,2,1,0:T(4,128)} %get-tuple-element.27), calls=%async_computation.1 | async-start | bytes 655360 | tf_op jit(solution)/shard_map/all_to_all | solution.py:340
  39.9 1.9 %collective-permute-start = (f32[8,5,4,128]{3,2,1,0:T(4,128)S(1)}, f32[8,5,4,128]{3,2,1,0:T(4,128)S(1)}, u32[]{:S(2)}, u32[]{:S(2)}) collective-permute-start(f32[8,5,4,128]{3,2,1,0:T(4,128)S(1)} %get-tuple-element.23.own_ref), channel_id=1, source_target_pairs={{0,1},{1,0},{2,3},{3,2},{4,5},{5,4},{6,7},{7,6},{8,9},{9,8},{10,11... | collective-permute-start | bytes 245768 | tf_op jit(solution)/shard_map/ppermute | solution.py:341
  41.9 1.2 %collective-permute-done.other_ref = f32[8,5,4,128]{3,2,1,0:T(4,128)S(1)} collective-permute-done((f32[8,5,4,128]{3,2,1,0:T(4,128)S(1)}, f32[8,5,4,128]{3,2,1,0:T(4,128)S(1)}, u32[]{:S(2)}, u32[]{:S(2)}) %collective-permute-start) | collective-permute-done | bytes 81952 | tf_op jit(solution)/shard_map/ppermute | solution.py:341
  43.1 1.1 %row_factors.1 = (f32[64,8,128]{2,1,0:T(8,128)S(1)}, bf16[64,128,128]{2,1,0:T(8,128)(2,1)S(1)}) custom-call(f32[8,5,4,128]{3,2,1,0:T(4,128)S(1)} %get-tuple-element.23.own_ref, f32[8,5,4,128]{3,2,1,0:T(4,128)S(1)} %collective-permute-done.other_ref, bf16[96,24]{1,0:T(8,128)(2,1)S(1)} %get-tuple-element.24.table_ref), custom_call_target="tpu_custom_call" | custom-call | flops 201326592 | bytes 4194304 | tf_op jit(solution)/shard_map/row_factors/pallas_call | solution.py:344
  44.2 0.0 copy-start.1
  44.3 4.5 %all-to-all-done.1 = f32[16,2,5,4,128]{4,3,2,1,0:T(4,128)S(1)} async-done(((f32[16,2,5,4,128]{4,3,2,1,0:T(4,128)}), f32[16,2,5,4,128]{4,3,2,1,0:T(4,128)S(1)}, u32[]{:S(2)}, u32[]{:S(2)}) %all-to-all-start.1) | async-done | bytes 327712 | tf_op jit(solution)/shard_map/all_to_all | solution.py:340
  48.8 6.0 %pair_forces.1 = (f32[8,3,4,128]{3,2,1,0:T(4,128)S(1)}, f32[8,3,4,128]{3,2,1,0:T(4,128)S(1)}, f32[4,8,3,4,128]{4,3,2,1,0:T(4,128)}) custom-call(s32[3,128]{1,0:T(4,128)S(1)} %get-tuple-element.21.pairs_ref, f32[64,8,128]{2,1,0:T(8,128)S(1)} %get-tuple-element.25.row_block, bf16[64,128,128]{2,1,0:T(8,128)(2,1)S(1)} %get-tuple-element.26.lhs_ref, ...), custom_call_target="tpu_custom_call" | custom-call | tf_op jit(solution)/shard_map/pair_forces/pallas_call | solution.py:358
  54.8 7.6 %all-to-all-start.2 = ((f32[16,2,3,4,128]{4,3,2,1,0:T(4,128)}), f32[16,2,3,4,128]{4,3,2,1,0:T(4,128)S(1)}, u32[]{:S(2)}, u32[]{:S(2)}) async-start(f32[16,2,3,4,128]{4,3,2,1,0:T(4,128)} %bitcast.7), calls=%async_computation.2 | async-start | bytes 393216 | tf_op jit(solution)/shard_map/all_to_all | solution.py:377
  62.4 1.9 %collective-permute-start.1 = (f32[8,3,4,128]{3,2,1,0:T(4,128)S(1)}, f32[8,3,4,128]{3,2,1,0:T(4,128)S(1)}, u32[]{:S(2)}, u32[]{:S(2)}) collective-permute-start(f32[8,3,4,128]{3,2,1,0:T(4,128)S(1)} %get-tuple-element.29), channel_id=1, source_target_pairs={{0,1},{1,0},{2,3},{3,2},{4,5},{5,4},{6,7},{7,6},{8,9},{9,8},{10,11... | collective-permute-start | bytes 147464 | tf_op jit(solution)/shard_map/ppermute | solution.py:376
  64.3 0.1 iota.21
  64.4 0.1 iota.22
  64.5 0.1 iota.26
  64.6 0.9 %collective-permute-done.1 = f32[8,3,4,128]{3,2,1,0:T(4,128)S(1)} collective-permute-done((f32[8,3,4,128]{3,2,1,0:T(4,128)S(1)}, f32[8,3,4,128]{3,2,1,0:T(4,128)S(1)}, u32[]{:S(2)}, u32[]{:S(2)}) %collective-permute-start.1) | collective-permute-done | bytes 49184 | tf_op jit(solution)/shard_map/ppermute | solution.py:376
  65.5 4.9 %all-to-all-done.2 = f32[16,2,3,4,128]{4,3,2,1,0:T(4,128)S(1)} async-done(((f32[16,2,3,4,128]{4,3,2,1,0:T(4,128)}), f32[16,2,3,4,128]{4,3,2,1,0:T(4,128)S(1)}, u32[]{:S(2)}, u32[]{:S(2)}) %all-to-all-start.2) | async-done | bytes 196640 | tf_op jit(solution)/shard_map/all_to_all | solution.py:377
  70.5 0.1 bitcast_select_fusion
  70.6 17.1 %all_to_all.20 = f32[16,3,4,128]{3,2,1,0:T(4,128)S(1)} all-to-all(f32[16,3,4,128]{3,2,1,0:T(4,128)S(1)} %bitcast_select_fusion), channel_id=1, replica_groups={{0,2,4,6,8,10,12,14,64,66,68,70,72,74,76,78},{1,3,5,7,9,11,13,15,65,67,..., dimensions={0} | all-to-all | bytes 196608 | tf_op jit(solution)/shard_map/all_to_all | solution.py:389
  87.7 0.0 copy-done.1
  87.7 0.6 multiply_add_fusion
  (9 shorter events, 0.1 us)
Async XLA Ops:
  2.0 30.1 %all-to-all-start = ((f32[16,5,4,128]{3,2,1,0:T(4,128)}), f32[16,5,4,128]{3,2,1,0:T(4,128)S(1)}, u32[]{:S(2)}, u32[]{:S(2)}) async-start(f32[16,5,4,128]{3,2,1,0:T(4,128)} %get-tuple-element.18), calls=%async_computation | async-start | bytes 327680 | tf_op jit(solution)/shard_map/all_to_all | solution.py:327
  19.5 0.7 copy-start
  32.9 15.9 %all-to-all-start.1 = ((f32[16,2,5,4,128]{4,3,2,1,0:T(4,128)}), f32[16,2,5,4,128]{4,3,2,1,0:T(4,128)S(1)}, u32[]{:S(2)}, u32[]{:S(2)}) async-start(f32[16,2,5,4,128]{4,3,2,1,0:T(4,128)} %get-tuple-element.27), calls=%async_computation.1 | async-start | bytes 655360 | tf_op jit(solution)/shard_map/all_to_all | solution.py:340
  39.9 3.2 %collective-permute-start = (f32[8,5,4,128]{3,2,1,0:T(4,128)S(1)}, f32[8,5,4,128]{3,2,1,0:T(4,128)S(1)}, u32[]{:S(2)}, u32[]{:S(2)}) collective-permute-start(f32[8,5,4,128]{3,2,1,0:T(4,128)S(1)} %get-tuple-element.23.own_ref), channel_id=1, source_target_pairs={{0,1},{1,0},{2,3},{3,2},{4,5},{5,4},{6,7},{7,6},{8,9},{9,8},{10,11... | collective-permute-start | bytes 245768 | tf_op jit(solution)/shard_map/ppermute | solution.py:341
  44.2 43.5 %copy-start.1 = (f32[3,512]{1,0:T(4,128)S(1)}, f32[3,512]{1,0:T(4,128)}, u32[]{:S(2)}) copy-start(f32[3,512]{1,0:T(4,128)} %vel_ref.1) | copy-start | bytes 18436
  54.8 15.7 %all-to-all-start.2 = ((f32[16,2,3,4,128]{4,3,2,1,0:T(4,128)}), f32[16,2,3,4,128]{4,3,2,1,0:T(4,128)S(1)}, u32[]{:S(2)}, u32[]{:S(2)}) async-start(f32[16,2,3,4,128]{4,3,2,1,0:T(4,128)} %bitcast.7), calls=%async_computation.2 | async-start | bytes 393216 | tf_op jit(solution)/shard_map/all_to_all | solution.py:377
  62.4 3.1 %collective-permute-start.1 = (f32[8,3,4,128]{3,2,1,0:T(4,128)S(1)}, f32[8,3,4,128]{3,2,1,0:T(4,128)S(1)}, u32[]{:S(2)}, u32[]{:S(2)}) collective-permute-start(f32[8,3,4,128]{3,2,1,0:T(4,128)S(1)} %get-tuple-element.29), channel_id=1, source_target_pairs={{0,1},{1,0},{2,3},{3,2},{4,5},{5,4},{6,7},{7,6},{8,9},{9,8},{10,11... | collective-permute-start | bytes 147464 | tf_op jit(solution)/shard_map/ppermute | solution.py:376
